TPU v7x, 128 devices: a whole 4x4x4 slice. The times are simulated.
128 devices in a mesh: expert: 32 (over z, y, core), group: 4 (over x).
Axes of the slice: x: 4, y: 4, z: 4, core: 2. Of those that a mesh axis runs over, the one named last changes fastest.
Arguments:
- tokens: bfloat16 [16384, 2048], P(('expert', 'group')), may hold values from -6 to 6
- low_tap: bfloat16 [16384, 2048], P(('expert', 'group')), may hold values from -6 to 6
- mid_tap: bfloat16 [16384, 2048], P(('expert', 'group')), may hold values from -6 to 6
- next_embed: bfloat16 [16384, 2048], P(('expert', 'group')), may hold values from -6 to 6
- expert_ids: int32 [16384, 8], P(('expert', 'group')), may hold values from 0 to 127, all different within a row; in each aligned block of 128 rows (0 to 127, 128 to 255, ...) at most 12 rows name the same one
- gate_weights: float32 [16384, 8], P(('expert', 'group')), may hold values from 0.02 to 0.3
- segments: int32 [16384], replicated, may hold values from 0 to 3, never falling along the last dimension, each value on 1 to 8192 neighbouring positions
- moe_gain: float32 [2048], replicated, may hold values from 0.1 to 1.9
- w_gate: bfloat16 [128, 2048, 768], P(('expert', 'group')), may hold values from -0.125 to 0.125
- w_up: bfloat16 [128, 2048, 768], P(('expert', 'group')), may hold values from -0.125 to 0.125
- w_down: bfloat16 [128, 768, 2048], P(('expert', 'group')), may hold values from -0.21875 to 0.21875
- merge_weight: bfloat16 [6144, 2048], P(None, 'group'), may hold values from -0.078125 to 0.078125
- embed_gain: float32 [2048], replicated, may hold values from 0.1 to 1.9
- merged_gain: float32 [2048], replicated, may hold values from 0.1 to 1.9
- w_query: bfloat16 [4096, 2048], P(None, 'group'), may hold values from -0.09375 to 0.09375
- w_kv: bfloat16 [4096, 2, 512], P(None, None, 'group'), may hold values from -0.09375 to 0.09375
- q_gain: float32 [128], replicated, may hold values from 2 to 3
- k_gain: float32 [128], replicated, may hold values from 2 to 3
Outputs:
- attended: bfloat16 [16384, 2048], P('expert', 'group')
Inputs may be any that keep to these rules, and one draw needn't show every extreme that they name: `expert_ids`: each row names 8 different experts; within the rows of one device no expert is named by more than 12 rows, a bound that some block reaches. `segments`: never falling along the sequence; each segment holds 1 to 8192 positions, one exactly that many.
All inputs are finite; a program needn't handle non-finite values.
Results may differ from a plain program's by a relative error of at most 0.03.
Values may be sent and summed in bfloat16 or wider, within the bound.
A program may use at most 128 MiB of HBM per device.

v0:
```python
import jax
import jax.numpy as jnp
from jax import lax
from jax.sharding import PartitionSpec as P

D = 2048
HD = 128
TOPK = 8
SEGS = 4


EPSILON = 1e-06
THETA = 1000000.0


def rms_scale(values, gain):
    values = values.astype(jnp.float32)
    return values * lax.rsqrt(jnp.mean(values * values, axis=-1, keepdims=True) + EPSILON) * gain


def rotate(values, positions):
    half = values.shape[-1] // 2
    freqs = jnp.power(THETA, -jnp.arange(half, dtype=jnp.float32) * 2.0 / values.shape[-1])
    angles = positions.astype(jnp.float32)[:, None] * freqs[None, :]
    cosine = jnp.concatenate([jnp.cos(angles), jnp.cos(angles)], axis=-1)[:, None, :]
    sine = jnp.concatenate([jnp.sin(angles), jnp.sin(angles)], axis=-1)[:, None, :]
    turned = jnp.concatenate([-values[..., half:], values[..., :half]], axis=-1)
    return values * cosine + turned * sine


def segment_positions(segments):
    labels = jnp.arange(SEGS, dtype=jnp.int32)
    member = (segments[:, None] == labels[None, :]).astype(jnp.int32)
    counts = jnp.sum(member, axis=0)
    starts = jnp.cumsum(counts) - counts
    return jnp.arange(segments.shape[0], dtype=jnp.int32) - jnp.sum(
        member * starts[None, :], axis=1
    )


def expert_ffn(rows, gate_mat, up_mat, down_mat):
    gate = jnp.dot(rows, gate_mat, preferred_element_type=jnp.float32)
    up = jnp.dot(rows, up_mat, preferred_element_type=jnp.float32)
    hidden = (jax.nn.silu(gate) * up).astype(jnp.bfloat16)
    return jnp.dot(hidden, down_mat, preferred_element_type=jnp.float32).astype(jnp.bfloat16)


def body(
    tokens,
    low_tap,
    mid_tap,
    next_embed,
    expert_ids,
    gate_weights,
    segments,
    moe_gain,
    w_gate,
    w_up,
    w_down,
    merge_weight,
    embed_gain,
    merged_gain,
    w_query,
    w_kv,
    q_gain,
    k_gain,
):
    n_expert = lax.axis_size("expert")
    n_group = lax.axis_size("group")
    devices = n_expert * n_group
    tok_rows = tokens.shape[0]
    capacity = 3 * tok_rows * TOPK // (2 * devices)
    normed = rms_scale(tokens, moe_gain).astype(jnp.bfloat16)
    flat_ids = expert_ids.reshape(-1)
    picks = flat_ids.shape[0]
    onehot = (flat_ids[:, None] == jnp.arange(devices, dtype=jnp.int32)[None, :]).astype(
        jnp.bfloat16
    )
    order = jnp.arange(picks, dtype=jnp.int32)
    earlier = (order[:, None] > order[None, :]).astype(jnp.bfloat16)
    ranks = jnp.dot(earlier, onehot, preferred_element_type=jnp.float32)
    slot_of = jnp.sum(ranks * onehot.astype(jnp.float32), axis=1).astype(jnp.int32)
    target = flat_ids * capacity + slot_of
    place = jnp.arange(devices * capacity, dtype=jnp.int32)[:, None] == target[None, :]
    place = jnp.any(place.reshape(devices * capacity, tok_rows, TOPK), axis=2).astype(jnp.bfloat16)
    packed = jnp.dot(place, normed, preferred_element_type=jnp.float32).astype(jnp.bfloat16)
    packed = packed.reshape(devices, capacity, D)
    items = lax.all_to_all(packed, ("expert", "group"), split_axis=0, concat_axis=0, tiled=True)
    rows = items.reshape(-1, items.shape[-1])
    answered = expert_ffn(rows, w_gate[0], w_up[0], w_down[0]).reshape(items.shape)
    returned = lax.all_to_all(
        answered, ("expert", "group"), split_axis=0, concat_axis=0, tiled=True
    )
    returned = returned.reshape(devices * capacity, D)
    picked = jnp.take(returned, target, axis=0).reshape(tok_rows, TOPK, D)
    mixed = jnp.einsum("tkd,tk->td", picked, gate_weights, preferred_element_type=jnp.float32)
    high = (tokens.astype(jnp.float32) + mixed).astype(jnp.bfloat16)
    low_rows, mid_rows, high_rows, embed_rows = (
        lax.all_gather(low_tap, "group", axis=0, tiled=True),
        lax.all_gather(mid_tap, "group", axis=0, tiled=True),
        lax.all_gather(high, "group", axis=0, tiled=True),
        lax.all_gather(next_embed, "group", axis=0, tiled=True),
    )
    stacked = jnp.concatenate([low_rows, mid_rows, high_rows], axis=1)
    merged_part = jnp.dot(stacked, merge_weight, preferred_element_type=jnp.float32).astype(
        jnp.bfloat16
    )
    merged = lax.all_gather(merged_part, "group", axis=1, tiled=True)
    joined = jnp.concatenate(
        [rms_scale(embed_rows, embed_gain), rms_scale(merged, merged_gain)], axis=1
    ).astype(jnp.bfloat16)
    block_rows = joined.shape[0]
    first = lax.axis_index("expert") * block_rows
    every_position = segment_positions(segments)
    my_positions = lax.dynamic_slice_in_dim(every_position, first, block_rows)
    my_segments = lax.dynamic_slice_in_dim(segments, first, block_rows)
    row_index = first + jnp.arange(block_rows, dtype=jnp.int32)
    query = jnp.dot(joined, w_query, preferred_element_type=jnp.float32).reshape(block_rows, -1, HD)
    query = rotate(rms_scale(query, q_gain), my_positions).astype(jnp.bfloat16)
    key = jnp.dot(joined, w_kv[:, 0, :], preferred_element_type=jnp.float32).reshape(
        block_rows, -1, HD
    )
    key = rotate(rms_scale(key, k_gain), my_positions).astype(jnp.bfloat16)
    value = jnp.dot(joined, w_kv[:, 1, :], preferred_element_type=jnp.float32).astype(jnp.bfloat16)
    kv_local = key.shape[1]
    q_local = query.shape[1]
    per_kv = q_local // kv_local
    paired = jnp.stack([key.reshape(block_rows, kv_local * HD), value], axis=0)
    grouped = query.reshape(block_rows, kv_local, per_kv, HD)
    scale = HD ** (-0.5)
    start_total = jnp.zeros((kv_local, per_kv, block_rows, HD), jnp.float32)
    start_denom = jnp.zeros((kv_local, per_kv, block_rows), jnp.float32)
    piece = lax.all_gather(paired, "expert", axis=1, tiled=True)
    count = piece.shape[1] // block_rows

    def step(index, inner):
        total, denom = inner
        offset = index * block_rows
        block = lax.dynamic_slice_in_dim(piece, offset, block_rows, 1).reshape(
            2, block_rows, kv_local, HD
        )
        key_index = offset + jnp.arange(block_rows, dtype=jnp.int32)
        key_seg = lax.dynamic_slice_in_dim(segments, offset, block_rows)
        allowed = (key_index[None, :] <= row_index[:, None]) & (
            key_seg[None, :] == my_segments[:, None]
        )
        scores = (
            jnp.einsum("qhgd,khd->hgqk", grouped, block[0], preferred_element_type=jnp.float32)
            * scale
        )
        weights = jnp.where(allowed[None, None], jnp.exp(scores), 0.0)
        total = total + jnp.einsum(
            "hgqk,khd->hgqd",
            weights.astype(jnp.bfloat16),
            block[1],
            preferred_element_type=jnp.float32,
        )
        denom = denom + jnp.sum(weights, axis=-1)
        return (total, denom)

    total, denom = lax.fori_loop(0, count, step, (start_total, start_denom))
    result = total / denom[..., None]
    return (
        jnp.transpose(result, (2, 0, 1, 3)).reshape(block_rows, q_local * HD).astype(jnp.bfloat16)
    )


def solution(mesh):
    return jax.shard_map(
        body,
        mesh=mesh,
        in_specs=(
            P(("expert", "group"), None),
            P(("expert", "group"), None),
            P(("expert", "group"), None),
            P(("expert", "group"), None),
            P(("expert", "group"), None),
            P(("expert", "group"), None),
            P(),
            P(),
            P(("expert", "group"), None, None),
            P(("expert", "group"), None, None),
            P(("expert", "group"), None, None),
            P(None, "group"),
            P(),
            P(),
            P(None, "group"),
            P(None, None, "group"),
            P(),
            P(),
        ),
        out_specs=P("expert", "group"),
        check_vma=False,
    )
```

profile of v0, /device:TPU:66, one launch (start us, length us, event | category | flops | bytes accessed | tf_op | source)
XLA Modules:
  0.0 807.6 jit_solution(4702539697536787441)
XLA Ops:
  9.1 5.6 fusion.28
  15.9 5.6 convolution_convert_fusion.1
  21.5 10.6 %reshape.351 = bf16[128,12,2048]{2,1,0:T(8,128)(2,1)} reshape(bf16[1536,2048]{1,0:T(8,128)(2,1)} %convolution_convert_fusion.1) | data formatting | bytes 12582912 | tf_op jit(solution)/shard_map/reshape | solution.py:87
  32.1 104.0 %all_to_all.10 = bf16[128,12,2048]{2,1,0:T(8,128)(2,1)} all-to-all(bf16[128,12,2048]{2,1,0:T(8,128)(2,1)} %reshape.351), channel_id=1, replica_groups=mesh['expert'=32,'group'=4] {'expert','group'}, dimensions={0} | all-to-all | bytes 12582912 | tf_op jit(solution)/shard_map/all_to_all | solution.py:88
  136.1 10.7 %reshape.352 = bf16[1536,2048]{1,0:T(8,128)(2,1)} reshape(bf16[128,12,2048]{2,1,0:T(8,128)(2,1)} %all_to_all.10) | data formatting | bytes 12582912 | tf_op jit(solution)/shard_map/reshape | solution.py:89
  146.8 8.2 %fusion.40 = f32[1536,768]{1,0:T(8,128)S(1)} fusion(bf16[1536,2048]{1,0:T(8,128)(2,1)} %reshape.352, bf16[1,2048,768]{2,1,0:T(8,128)(2,1)} %param.28), kind=kOutput, calls=%fused_computation.53 | convolution fusion | flops 4831838208 | bytes 14155776 | tf_op jit(solution)/shard_map/dot_general | solution.py:42
  155.0 5.6 multiply_convert_fusion
  160.7 7.1 convolution_convert_fusion
  167.8 10.6 %reshape.353 = bf16[128,12,2048]{2,1,0:T(8,128)(2,1)} reshape(bf16[1536,2048]{1,0:T(8,128)(2,1)} %convolution_convert_fusion) | data formatting | bytes 12582912 | tf_op jit(solution)/shard_map/reshape | solution.py:90
  178.4 10.2 %all-to-all-start.1 = ((bf16[128,12,2048]{2,1,0:T(8,128)(2,1)}), bf16[128,12,2048]{2,1,0:T(8,128)(2,1)}, u32[]{:S(2)}, u32[]{:S(2)}) async-start(bf16[128,12,2048]{2,1,0:T(8,128)(2,1)} %reshape.353), calls=%async_computation.1 | async-start | bytes 16777216 | tf_op jit(solution)/shard_map/all_to_all | solution.py:91
  190.7 125.6 %all-to-all-done.1 = bf16[128,12,2048]{2,1,0:T(8,128)(2,1)} async-done(((bf16[128,12,2048]{2,1,0:T(8,128)(2,1)}), bf16[128,12,2048]{2,1,0:T(8,128)(2,1)}, u32[]{:S(2)}, u32[]{:S(2)}) %all-to-all-start.1) | async-done | bytes 6291488 | tf_op jit(solution)/shard_map/all_to_all | solution.py:91
  316.3 10.7 %reshape.354 = bf16[1536,2048]{1,0:T(8,128)(2,1)} reshape(bf16[128,12,2048]{2,1,0:T(8,128)(2,1)} %all-to-all-done.1) | data formatting | bytes 12582912 | tf_op jit(solution)/shard_map/reshape | solution.py:94
  327.0 12.4 %gather_fusion = bf16[1024,2048]{1,0:T(8,128)(2,1)} fusion(bf16[1536,2048]{1,0:T(8,128)(2,1)} %reshape.354, s32[1024]{0:T(1024)S(1)} %broadcast_clamp_fusion), kind=kCustom, calls=%fused_computation | custom fusion | bytes 8392704 | tf_op jit(solution)/shard_map/jit(_take)/gather | solution.py:95
  344.8 30.1 %all-gather.13.cloned.1.call-done = bf16[512,2048]{1,0:T(8,128)(2,1)} async-done(((bf16[128,2048]{1,0:T(8,128)(2,1)}), bf16[512,2048]{1,0:T(8,128)(2,1)}) %all-gather.13.cloned.1.call-update) | async-done | bytes 2097168 | tf_op jit(solution)/shard_map/all_gather | solution.py:101
  374.9 8.9 %fusion.43 = bf16[512,512]{1,0:T(8,128)(2,1)} fusion(bf16[6144,512]{1,0:T(8,128)(2,1)} %param.31, bf16[512,2048]{1,0:T(8,128)(2,1)} %all-gather.13.cloned.1.call-done, bf16[512,2048]{1,0:T(8,128)(2,1)} %all-gather.11.cloned.1.call-done, bf16[512,2048]{1,0:T(8,128)(2,1)} %all-gather.9.cloned.1.call-done), kind=kOutput, calls=%fused_computation.59 | convolution fusion | flops 3240361984 | bytes 13107200 | tf_op jit(solution)/shard_map/dot_general | solution.py:105
  389.7 17.7 %all-gather.7.cloned.1.call-done = bf16[512,2048]{1,0:T(8,128)(2,1)} async-done(((bf16[128,2048]{1,0:T(8,128)(2,1)}), bf16[512,2048]{1,0:T(8,128)(2,1)}) %all-gather.7.cloned.1.call-update) | async-done | bytes 2097168 | tf_op jit(solution)/shard_map/all_gather | solution.py:102
  411.6 28.1 %all-gather.15.cloned.1.call-done = bf16[512,2048]{1,0:T(8,128)(2,1)} async-done(((bf16[512,512]{1,0:T(8,128)(2,1)}), bf16[512,2048]{1,0:T(8,128)(2,1)}) %all-gather.15.cloned.1.call-update) | async-done | bytes 2097168 | tf_op jit(solution)/shard_map/all_gather | solution.py:108
  450.0 5.2 multiply_reduce_fusion
  457.4 50.6 %all-gather.17.cloned.1.call-done = bf16[2,16384,128]{1,2,0:T(8,128)(2,1)} async-done(((bf16[2,512,128]{1,2,0:T(8,128)(2,1)}), bf16[2,16384,128]{1,2,0:T(8,128)(2,1)}) %all-gather.17.cloned.1.call-update) | async-done | bytes 8388624 | tf_op jit(solution)/shard_map/all_gather | solution.py:133
  508.0 289.7 %while.16 = (s32[]{:T(128)}, f32[1,4,512,128]{3,2,1,0:T(8,128)}, f32[1,4,512]{2,1,0:T(4,128)S(1)}, s32[16384]{0:T(1024)S(1)}, s32[512]{0:T(512)S(1)}, /*index=5*...) while((s32[]{:T(128)}, f32[1,4,512,128]{3,2,1,0:T(8,128)}, ...), condition=%wide.region_12.13_spmd.clone, body=%wide.region_10.12_spmd.clone.sunk | while | flops 544476160 | bytes 12107994 | solution.py:161
  521.1 4.7 fusion.92
  530.2 4.7 fusion.92
  539.2 4.7 fusion.92
  548.3 4.7 fusion.92
  557.3 4.7 fusion.92
  566.4 4.7 fusion.92
  575.5 4.7 fusion.92
  584.5 4.7 fusion.92
  593.6 4.7 fusion.92
  602.7 4.7 fusion.92
  611.7 4.7 fusion.92
  620.8 4.7 fusion.92
  629.9 4.7 fusion.92
  638.9 4.7 fusion.92
  648.0 4.7 fusion.92
  657.1 4.7 fusion.92
  666.1 4.7 fusion.92
  675.2 4.7 fusion.92
  684.3 4.7 fusion.92
  693.3 4.7 fusion.92
  702.4 4.7 fusion.92
  711.5 4.7 fusion.92
  720.5 4.7 fusion.92
  729.6 4.7 fusion.92
  738.7 4.7 fusion.92
  747.7 4.7 fusion.92
  756.8 4.7 fusion.92
  765.8 4.7 fusion.92
  (265 shorter events, 193.7 us)
Async XLA Ops:
  6.5 154.1 %copy-start = (bf16[1,768,2048]{2,1,0:T(8,128)(2,1)S(1)}, bf16[1,768,2048]{2,1,0:T(8,128)(2,1)}, u32[]{:S(2)}) copy-start(bf16[1,768,2048]{2,1,0:T(8,128)(2,1)} %param.30) | copy-start | bytes 9437188
  146.8 8.2 %copy-start.3 = (bf16[1536,2048]{1,0:T(8,128)(2,1)S(1)}, bf16[1536,2048]{1,0:T(8,128)(2,1)}, u32[]{:S(2)}) copy-start(bf16[1536,2048]{1,0:T(8,128)(2,1)} %reshape.352) | copy-start | bytes 18874372
  146.8 8.2 %copy-start.16 = (bf16[1,2048,768]{2,1,0:T(8,128)(2,1)S(1)}, bf16[1,2048,768]{2,1,0:T(8,128)(2,1)}, u32[]{:S(2)}) copy-start(bf16[1,2048,768]{2,1,0:T(8,128)(2,1)} %param.29) | copy-start | bytes 9437188
  178.4 11.8 %copy-start.10 = (s32[128,8]{0,1:T(8,128)S(1)}, s32[128,8]{0,1:T(8,128)}, u32[]{:S(2)}) copy-start(s32[128,8]{0,1:T(8,128)} %param.24) | copy-start | bytes 12292
  178.4 12.1 %copy-start.13 = (f32[128,8]{0,1:T(8,128)S(1)}, f32[128,8]{0,1:T(8,128)}, u32[]{:S(2)}) copy-start(f32[128,8]{0,1:T(8,128)} %param.25) | copy-start | bytes 12292
  178.4 137.9 %all-to-all-start.1 = ((bf16[128,12,2048]{2,1,0:T(8,128)(2,1)}), bf16[128,12,2048]{2,1,0:T(8,128)(2,1)}, u32[]{:S(2)}, u32[]{:S(2)}) async-start(bf16[128,12,2048]{2,1,0:T(8,128)(2,1)} %reshape.353), calls=%async_computation.1 | async-start | bytes 16777216 | tf_op jit(solution)/shard_map/all_to_all | solution.py:91
  188.6 156.2 %all-gather.11.cloned.1.call-start = ((), (), s32[]{:S(2)}) async-start(), calls=%async_computation.4 | async-start | bytes 2621440 | tf_op jit(solution)/shard_map/all_gather | solution.py:100
  189.3 155.5 %all-gather.9.cloned.1.call-start = ((), (), s32[]{:S(2)}) async-start(), calls=%async_computation.3 | async-start | bytes 2621440 | tf_op jit(solution)/shard_map/all_gather | solution.py:99
  190.1 184.8 %all-gather.13.cloned.1.call-start = ((), (), s32[]{:S(2)}) async-start(), calls=%async_computation.5 | async-start | bytes 2621440 | tf_op jit(solution)/shard_map/all_gather | solution.py:101
  339.4 3.6 copy-start.4
  344.1 63.2 %all-gather.7.cloned.1.call-start = ((), (), s32[]{:S(2)}) async-start(), calls=%async_computation.2 | async-start | bytes 2621440 | tf_op jit(solution)/shard_map/all_gather | solution.py:102
  344.7 39.2 %copy-start.9 = (s32[16384]{0:T(1024)S(1)}, s32[16384]{0:T(1024)}, u32[]{:S(2)}) copy-start(s32[16384]{0:T(1024)} %param.26) | copy-start | bytes 196612
  344.7 40.5 %copy-start.2 = (bf16[4096,2,128]{2,1,0:T(2,128)(2,1)S(1)}, bf16[4096,2,128]{2,1,0:T(2,128)(2,1)}, u32[]{:S(2)}) copy-start(bf16[4096,2,128]{2,1,0:T(2,128)(2,1)} %param.35) | copy-start | bytes 6291460
  344.7 95.0 %all-gather.15.cloned.1.call-start = ((), (), s32[]{:S(2)}) async-start(), calls=%async_computation.6 | async-start | bytes 2621440 | tf_op jit(solution)/shard_map/all_gather | solution.py:108
  383.8 124.2 %all-gather.17.cloned.1.call-start = ((), (), s32[]{:S(2)}) async-start(), calls=%async_computation.7 | async-start | bytes 8650752 | tf_op jit(solution)/shard_map/all_gather | solution.py:133
  385.2 24.2 %copy-start.11 = (f32[2048]{0:T(1024)S(1)}, f32[2048]{0:T(1024)}, u32[]{:S(2)}) copy-start(f32[2048]{0:T(1024)} %param.32) | copy-start | bytes 24580
  389.7 52.3 %copy-start.12 = (f32[2048]{0:T(1024)S(1)}, f32[2048]{0:T(1024)}, u32[]{:S(2)}) copy-start(f32[2048]{0:T(1024)} %param.33) | copy-start | bytes 24580
  439.7 4.4 copy-start.7
  444.1 1.7 copy-start.5
  444.1 1.6 copy-start.14
  444.1 2.4 copy-start.6
  455.2 0.7 copy-start.15
  455.8 1.0 copy-start.8
  797.8 3.0 copy-start.1
Sparse Core Ops, SparseCore 0:
  191.1 63.6 all-gather.10
  256.4 55.2 all-gather.8
  344.2 30.6 all-gather.12
  376.4 30.8 all-gather.6
  408.9 30.7 all-gather.14
  449.0 58.9 all-gather.16
where the time goes:
time: 813 us; the launch traced here: 808 us
  matrix products  325 us (40%)
  waiting for transfers between devices  254 us (31%)
  blocking collectives  104 us (13%)
  local copies, waits for them, and re-layouts  67.5 us (8%)
  other arithmetic  31.9 us (4%)
  between operations  13.9 us (2%)
  starting transfers between devices  10.5 us (1%)
    dot_general x32, matrix products, step(): jnp.einsum('hgqk,khd->hgqd', weights.astype(jnp.bfloat16), block[1], pref...  150 us
    dot_general x32, matrix products, step(): jnp.einsum('qhgd,khd->hgqk', grouped, block[0], preferred_element_type=jn...  127 us
    all_to_all x1, waiting for transfers between devices, body(): lax.all_to_all(answered, ('expert', 'group'), split_axis=0, concat_axis=0...  126 us
    all_to_all x1, blocking collectives, body(): lax.all_to_all(packed, ('expert', 'group'), split_axis=0, concat_axis=0,...  104 us
    all_gather x1, waiting for transfers between devices, body(): piece = lax.all_gather(paired, 'expert', axis=1, tiled=True)  50.6 us
    all_gather x1, waiting for transfers between devices, body(): lax.all_gather(high, 'group', axis=0, tiled=True)  30.1 us
    all_gather x1, waiting for transfers between devices, body(): merged = lax.all_gather(merged_part, 'group', axis=1, tiled=True)  28.1 us
    all_gather x1, waiting for transfers between devices, body(): lax.all_gather(next_embed, 'group', axis=0, tiled=True)  17.7 us
  transfers between devices with their start and end apart: 7, of which 5 were waited for; matrix products, arithmetic and copies ran while one was open for 7% of the time, Pallas kernels for 0%

commit v1 on v0

--- a/solution.py
+++ b/solution.py
@@ -1,6 +1,8 @@
 import jax
 import jax.numpy as jnp
 from jax import lax
+from jax.experimental import pallas as pl
+from jax.experimental.pallas import tpu as pltpu
 from jax.sharding import PartitionSpec as P
 
 D = 2048
@@ -11,6 +13,7 @@
 
 EPSILON = 1e-06
 THETA = 1000000.0
+LOG2E = 1.4426950408889634
 
 
 def rms_scale(values, gain):
@@ -43,6 +46,61 @@
     up = jnp.dot(rows, up_mat, preferred_element_type=jnp.float32)
     hidden = (jax.nn.silu(gate) * up).astype(jnp.bfloat16)
     return jnp.dot(hidden, down_mat, preferred_element_type=jnp.float32).astype(jnp.bfloat16)
+
+
+def attend_kernel(bounds, query, pairs, row_start, out, total):
+    heads, rows, _ = query.shape
+    first_start, low, mine = bounds[0], bounds[1], bounds[2]
+    total[...] = jnp.zeros_like(total)
+
+    def add_block(index, masked):
+        key = pairs[index, 0]
+        value = jnp.concatenate([pairs[index, 1], jnp.ones((rows, HD), jnp.bfloat16)], axis=1)
+        if masked:
+            row = mine * rows + lax.broadcasted_iota(jnp.int32, (rows, rows), 0)
+            col = index * rows + lax.broadcasted_iota(jnp.int32, (rows, rows), 1)
+            allowed = (col <= row) & (col >= row_start[...])
+        for head in range(heads):
+            scores = lax.dot_general(
+                query[head], key, (((1,), (1,)), ((), ())), preferred_element_type=jnp.float32
+            )
+            weights = jnp.exp2(scores)
+            if masked:
+                weights = jnp.where(allowed, weights, 0.0)
+            total[head] += jnp.dot(
+                weights.astype(jnp.bfloat16), value, preferred_element_type=jnp.float32
+            )
+
+    @pl.loop(low + 1, mine)
+    def _(index):
+        add_block(index, False)
+
+    same = row_start[...] == first_start
+    for head in range(heads):
+        total[head] = jnp.where(same, total[head], 0.0)
+
+    @pl.loop(0, jnp.where(low < mine, 2, 1))
+    def _(index):
+        add_block(jnp.where(index == 0, mine, low), True)
+
+    for head in range(heads):
+        out[:, head * HD : (head + 1) * HD] = (
+            total[head, :, :HD] / total[head, :, HD:]
+        ).astype(out.dtype)
+
+
+def attend(bounds, query, pairs, row_start):
+    rows, heads, _ = query.shape
+    vmem = pl.BlockSpec(memory_space=pltpu.VMEM)
+    return pl.pallas_call(
+        attend_kernel,
+        out_shape=jax.ShapeDtypeStruct((rows, heads * HD), jnp.bfloat16),
+        in_specs=[pl.BlockSpec(memory_space=pltpu.SMEM), vmem, vmem, vmem],
+        out_specs=vmem,
+        scratch_shapes=[pltpu.VMEM((heads, rows, 2 * HD), jnp.float32)],
+        compiler_params=pltpu.CompilerParams(vmem_limit_bytes=48 << 20),
+        name="attend",
+    )(bounds, jnp.transpose(query, (1, 0, 2)), pairs, row_start)
 
 
 def body(
@@ -116,53 +174,19 @@
     my_segments = lax.dynamic_slice_in_dim(segments, first, block_rows)
     row_index = first + jnp.arange(block_rows, dtype=jnp.int32)
     query = jnp.dot(joined, w_query, preferred_element_type=jnp.float32).reshape(block_rows, -1, HD)
-    query = rotate(rms_scale(query, q_gain), my_positions).astype(jnp.bfloat16)
+    query = rotate(rms_scale(query, q_gain), my_positions)
     key = jnp.dot(joined, w_kv[:, 0, :], preferred_element_type=jnp.float32).reshape(
         block_rows, -1, HD
     )
     key = rotate(rms_scale(key, k_gain), my_positions).astype(jnp.bfloat16)
     value = jnp.dot(joined, w_kv[:, 1, :], preferred_element_type=jnp.float32).astype(jnp.bfloat16)
-    kv_local = key.shape[1]
-    q_local = query.shape[1]
-    per_kv = q_local // kv_local
-    paired = jnp.stack([key.reshape(block_rows, kv_local * HD), value], axis=0)
-    grouped = query.reshape(block_rows, kv_local, per_kv, HD)
-    scale = HD ** (-0.5)
-    start_total = jnp.zeros((kv_local, per_kv, block_rows, HD), jnp.float32)
-    start_denom = jnp.zeros((kv_local, per_kv, block_rows), jnp.float32)
-    piece = lax.all_gather(paired, "expert", axis=1, tiled=True)
-    count = piece.shape[1] // block_rows
-
-    def step(index, inner):
-        total, denom = inner
-        offset = index * block_rows
-        block = lax.dynamic_slice_in_dim(piece, offset, block_rows, 1).reshape(
-            2, block_rows, kv_local, HD
-        )
-        key_index = offset + jnp.arange(block_rows, dtype=jnp.int32)
-        key_seg = lax.dynamic_slice_in_dim(segments, offset, block_rows)
-        allowed = (key_index[None, :] <= row_index[:, None]) & (
-            key_seg[None, :] == my_segments[:, None]
-        )
-        scores = (
-            jnp.einsum("qhgd,khd->hgqk", grouped, block[0], preferred_element_type=jnp.float32)
-            * scale
-        )
-        weights = jnp.where(allowed[None, None], jnp.exp(scores), 0.0)
-        total = total + jnp.einsum(
-            "hgqk,khd->hgqd",
-            weights.astype(jnp.bfloat16),
-            block[1],
-            preferred_element_type=jnp.float32,
-        )
-        denom = denom + jnp.sum(weights, axis=-1)
-        return (total, denom)
-
-    total, denom = lax.fori_loop(0, count, step, (start_total, start_denom))
-    result = total / denom[..., None]
-    return (
-        jnp.transpose(result, (2, 0, 1, 3)).reshape(block_rows, q_local * HD).astype(jnp.bfloat16)
-    )
+    scale = HD ** (-0.5) * LOG2E
+    scaled = (query * scale).astype(jnp.bfloat16)
+    paired = jnp.stack([key.reshape(block_rows, HD), value], axis=0)
+    gathered = lax.all_gather(paired, "expert", axis=0)
+    row_start = (row_index - my_positions)[:, None]
+    bounds = jnp.stack([row_start[0, 0], row_start[0, 0] // block_rows, lax.axis_index("expert")])
+    return attend(bounds, scaled, gathered, row_start)
 
 
 def solution(mesh):

time: 813 us -> 539 us (0.66)
  the two profiles are of different devices: /device:TPU:66 before, /device:TPU:57 now
where the time goes in v1:
time: 539 us; the launch traced here: 537 us
  waiting for transfers between devices  243 us (45%)
  blocking collectives  104 us (19%)
  local copies, waits for them, and re-layouts  66.6 us (12%)
  matrix products  47.9 us (9%)
  Pallas kernels  26.5 us (5%)
  other arithmetic  21.6 us (4%)
  between operations  16.5 us (3%)
  starting transfers between devices  11.2 us (2%)
    all_to_all x1, waiting for transfers between devices, body(): lax.all_to_all(answered, ('expert', 'group'), split_axis=0, concat_axis=0...  127 us
    all_to_all x1, blocking collectives, body(): lax.all_to_all(packed, ('expert', 'group'), split_axis=0, concat_axis=0,...  104 us
    all_gather x1, waiting for transfers between devices, body(): gathered = lax.all_gather(paired, 'expert', axis=0)  38.5 us
    all_gather x1, waiting for transfers between devices, body(): lax.all_gather(high, 'group', axis=0, tiled=True)  29.6 us
    all_gather x1, waiting for transfers between devices, body(): merged = lax.all_gather(merged_part, 'group', axis=1, tiled=True)  28.2 us
    pallas_call x1, Pallas kernels, attend(): pl.pallas_call(attend_kernel, out_shape=jax.ShapeDtypeStruct((rows, heads...  26.5 us
    all_gather x1, waiting for transfers between devices, body(): lax.all_gather(next_embed, 'group', axis=0, tiled=True)  17.6 us
    gather x1, local copies, waits for them, and re-layouts, body(): picked = jnp.take(returned, target, axis=0).reshape(tok_rows, TOPK, D)  12.4 us
  transfers between devices with their start and end apart: 7, of which 5 were waited for; matrix products, arithmetic and copies ran while one was open for 11% of the time, Pallas kernels for 0%

profile of v1, /device:TPU:57, one launch (start us, length us, event | category | flops | bytes accessed | tf_op | source)
XLA Modules:
  0.0 536.9 jit_solution(1206139062292503821)
XLA Ops:
  6.5 0.9 copy.56
  7.6 0.6 fusion.28
  8.3 0.7 compare_and_fusion
  9.1 5.6 %fusion.6 = pred[1536,128]{1,0:T(8,128)(4,1)S(1)} fusion(s32[128,8]{0,1:T(8,128)S(1)} %get-tuple-element.6), kind=kLoop, calls=%fused_computation.10 | loop fusion | flops 2949120 | bytes 200704 | tf_op jit(solution)/shard_map/reduce_or | solution.py:143
  14.6 1.2 fusion.31
  15.9 5.6 %convolution_convert_fusion.1 = bf16[1536,2048]{1,0:T(8,128)(2,1)} fusion(pred[1536,128]{1,0:T(8,128)(4,1)S(1)} %fusion.6, bf16[128,2048]{1,0:T(8,128)(2,1)} %param.18, f32[2048]{0:T(1024)} %param.25, f32[128]{0:T(128)S(1)} %add_rsqrt_fusion.4), kind=kOutput, calls=%fused_computation.2 | convolution fusion | flops 809500672 | bytes 7021056 | tf_op jit(solution)/shard_map/dot_general | solution.py:144
  21.5 10.6 %reshape.192 = bf16[128,12,2048]{2,1,0:T(8,128)(2,1)} reshape(bf16[1536,2048]{1,0:T(8,128)(2,1)} %convolution_convert_fusion.1) | data formatting | bytes 12582912 | tf_op jit(solution)/shard_map/reshape | solution.py:145
  32.1 103.9 %all_to_all.10 = bf16[128,12,2048]{2,1,0:T(8,128)(2,1)} all-to-all(bf16[128,12,2048]{2,1,0:T(8,128)(2,1)} %reshape.192), channel_id=1, replica_groups=mesh['expert'=32,'group'=4] {'expert','group'}, dimensions={0} | all-to-all | bytes 12582912 | tf_op jit(solution)/shard_map/all_to_all | solution.py:146
  136.0 10.7 %reshape.193 = bf16[1536,2048]{1,0:T(8,128)(2,1)} reshape(bf16[128,12,2048]{2,1,0:T(8,128)(2,1)} %all_to_all.10) | data formatting | bytes 12582912 | tf_op jit(solution)/shard_map/reshape | solution.py:147
  146.7 8.2 %fusion.18 = f32[1536,768]{1,0:T(8,128)S(1)} fusion(bf16[1536,2048]{1,0:T(8,128)(2,1)} %reshape.193, bf16[1,2048,768]{2,1,0:T(8,128)(2,1)} %param.26), kind=kOutput, calls=%fused_computation.30 | convolution fusion | flops 4831838208 | bytes 14155776 | tf_op jit(solution)/shard_map/dot_general | solution.py:45
  155.0 5.6 %multiply_convert_fusion = bf16[1536,768]{1,0:T(8,128)(2,1)S(1)} fusion(f32[1536,768]{1,0:T(8,128)S(1)} %fusion.18, bf16[1536,2048]{1,0:T(8,128)(2,1)S(1)} %copy-done.4, bf16[1,2048,768]{2,1,0:T(8,128)(2,1)S(1)} %copy-done.18), kind=kOutput, calls=%fused_computation.15 | convolution fusion | flops 4838916096 | bytes 16515072 | tf_op jit(solution)/shard_map/dot_general | solution.py:46
  160.6 7.1 %convolution_convert_fusion = bf16[1536,2048]{1,0:T(8,128)(2,1)} fusion(bf16[1536,768]{1,0:T(8,128)(2,1)S(1)} %multiply_convert_fusion, bf16[1,768,2048]{2,1,0:T(8,128)(2,1)S(1)} %copy-done), kind=kOutput, calls=%fused_computation.1 | convolution fusion | flops 4834983936 | bytes 11796480 | tf_op jit(solution)/shard_map/dot_general | solution.py:48
  167.7 10.6 %reshape.194 = bf16[128,12,2048]{2,1,0:T(8,128)(2,1)} reshape(bf16[1536,2048]{1,0:T(8,128)(2,1)} %convolution_convert_fusion) | data formatting | bytes 12582912 | tf_op jit(solution)/shard_map/reshape | solution.py:148
  178.3 10.8 %all-to-all-start.1 = ((bf16[128,12,2048]{2,1,0:T(8,128)(2,1)}), bf16[128,12,2048]{2,1,0:T(8,128)(2,1)}, u32[]{:S(2)}, u32[]{:S(2)}) async-start(bf16[128,12,2048]{2,1,0:T(8,128)(2,1)} %reshape.194), calls=%async_computation.1 | async-start | bytes 16777216 | tf_op jit(solution)/shard_map/all_to_all | solution.py:149
  189.1 0.7 all-gather.10.cloned.1.call-update
  189.8 0.7 all-gather.12.cloned.1.call-update
  191.1 126.8 %all-to-all-done.1 = bf16[128,12,2048]{2,1,0:T(8,128)(2,1)} async-done(((bf16[128,12,2048]{2,1,0:T(8,128)(2,1)}), bf16[128,12,2048]{2,1,0:T(8,128)(2,1)}, u32[]{:S(2)}, u32[]{:S(2)}) %all-to-all-start.1) | async-done | bytes 6291488 | tf_op jit(solution)/shard_map/all_to_all | solution.py:149
  317.9 10.7 %reshape.195 = bf16[1536,2048]{1,0:T(8,128)(2,1)} reshape(bf16[128,12,2048]{2,1,0:T(8,128)(2,1)} %all-to-all-done.1) | data formatting | bytes 12582912 | tf_op jit(solution)/shard_map/reshape | solution.py:152
  328.6 12.4 %gather_fusion = bf16[1024,2048]{1,0:T(8,128)(2,1)} fusion(bf16[1536,2048]{1,0:T(8,128)(2,1)} %reshape.195, s32[1024]{0:T(1024)S(1)} %broadcast_clamp_fusion), kind=kCustom, calls=%fused_computation | custom fusion | bytes 8392704 | tf_op jit(solution)/shard_map/jit(_take)/gather | solution.py:153
  341.0 3.6 fusion.13
  344.6 1.1 fusion.34
  345.8 0.5 all-gather.8.cloned.1.call-update
  346.5 29.6 %all-gather.14.cloned.1.call-done = bf16[512,2048]{1,0:T(8,128)(2,1)} async-done(((bf16[128,2048]{1,0:T(8,128)(2,1)}), bf16[512,2048]{1,0:T(8,128)(2,1)}) %all-gather.14.cloned.1.call-update) | async-done | bytes 2097168 | tf_op jit(solution)/shard_map/all_gather | solution.py:159
  376.0 8.9 %fusion.21 = bf16[512,512]{1,0:T(8,128)(2,1)} fusion(bf16[6144,512]{1,0:T(8,128)(2,1)} %param.29, bf16[512,2048]{1,0:T(8,128)(2,1)} %all-gather.14.cloned.1.call-done, bf16[512,2048]{1,0:T(8,128)(2,1)} %all-gather.12.cloned.1.call-done, bf16[512,2048]{1,0:T(8,128)(2,1)} %all-gather.10.cloned.1.call-done), kind=kOutput, calls=%fused_computation.36 | convolution fusion | flops 3240361984 | bytes 13107200 | tf_op jit(solution)/shard_map/dot_general | solution.py:163
  386.0 0.5 multiply_cosine_fusion
  386.6 4.2 fusion.57
  390.8 17.6 %all-gather.8.cloned.1.call-done = bf16[512,2048]{1,0:T(8,128)(2,1)} async-done(((bf16[128,2048]{1,0:T(8,128)(2,1)}), bf16[512,2048]{1,0:T(8,128)(2,1)}) %all-gather.8.cloned.1.call-update) | async-done | bytes 2097168 | tf_op jit(solution)/shard_map/all_gather | solution.py:160
  408.4 2.1 fusion.7
  410.5 2.1 fusion.9
  412.7 28.2 %all-gather.16.cloned.1.call-done = bf16[512,2048]{1,0:T(8,128)(2,1)} async-done(((bf16[512,512]{1,0:T(8,128)(2,1)}), bf16[512,2048]{1,0:T(8,128)(2,1)}) %all-gather.16.cloned.1.call-update) | async-done | bytes 2097168 | tf_op jit(solution)/shard_map/all_gather | solution.py:166
  440.8 2.2 fusion.10
  443.1 2.1 fusion.12
  445.3 1.6 multiply_reduce_fusion.1
  447.0 0.6 copy-done.7
  447.6 1.5 fusion.30
  449.3 0.9 copy.66
  450.2 0.5 slice.23
  453.5 0.7 pad_add_fusion.bounds
  454.2 0.9 copy.61
  455.0 0.8 copy.62
  455.9 5.2 multiply_reduce_fusion
  461.1 0.3 copy.60
  461.5 0.3 multiply_multiply_fusion
  461.8 0.3 slice_negate_fusion
  462.5 1.4 fusion.38.query
  463.9 38.5 %all-gather.18.cloned.1.call-done = bf16[64,512,128]{2,1,0:T(8,128)(2,1)} async-done(((bf16[2,512,128]{2,1,0:T(8,128)(2,1)}), bf16[64,512,128]{2,1,0:T(8,128)(2,1)}) %all-gather.18.cloned.1.call-update) | async-done | bytes 8388624 | tf_op jit(solution)/shard_map/all_gather | solution.py:186
  502.4 1.2 copy-done.2
  503.5 26.5 %attend.1 = bf16[512,512]{1,0:T(8,128)(2,1)} custom-call(s32[3]{0:T(128)S(1)} %pad_add_fusion.bounds, bf16[4,512,128]{2,1,0:T(8,128)(2,1)S(1)} %copy-done.2, bf16[32,2,512,128]{3,2,1,0:T(8,128)(2,1)} %bitcast.54, s32[512,1]{1,0:T(8,128)S(1)} %copy.67.row_start), custom_call_target="tpu_custom_call" | custom-call | tf_op jit(solution)/shard_map/attend/pallas_call | solution.py:95
  (74 shorter events, 2.8 us)
Async XLA Ops:
  6.5 154.1 %copy-start = (bf16[1,768,2048]{2,1,0:T(8,128)(2,1)S(1)}, bf16[1,768,2048]{2,1,0:T(8,128)(2,1)}, u32[]{:S(2)}) copy-start(bf16[1,768,2048]{2,1,0:T(8,128)(2,1)} %param.28) | copy-start | bytes 9437188
  146.7 8.2 %copy-start.4 = (bf16[1536,2048]{1,0:T(8,128)(2,1)S(1)}, bf16[1536,2048]{1,0:T(8,128)(2,1)}, u32[]{:S(2)}) copy-start(bf16[1536,2048]{1,0:T(8,128)(2,1)} %reshape.193) | copy-start | bytes 18874372
  146.7 8.2 %copy-start.18 = (bf16[1,2048,768]{2,1,0:T(8,128)(2,1)S(1)}, bf16[1,2048,768]{2,1,0:T(8,128)(2,1)}, u32[]{:S(2)}) copy-start(bf16[1,2048,768]{2,1,0:T(8,128)(2,1)} %param.27) | copy-start | bytes 9437188
  178.3 12.3 %copy-start.12 = (s32[128,8]{0,1:T(8,128)S(1)}, s32[128,8]{0,1:T(8,128)}, u32[]{:S(2)}) copy-start(s32[128,8]{0,1:T(8,128)} %param.22) | copy-start | bytes 12292
  178.3 12.6 %copy-start.15 = (f32[128,8]{0,1:T(8,128)S(1)}, f32[128,8]{0,1:T(8,128)}, u32[]{:S(2)}) copy-start(f32[128,8]{0,1:T(8,128)} %param.23) | copy-start | bytes 12292
  178.3 139.6 %all-to-all-start.1 = ((bf16[128,12,2048]{2,1,0:T(8,128)(2,1)}), bf16[128,12,2048]{2,1,0:T(8,128)(2,1)}, u32[]{:S(2)}, u32[]{:S(2)}) async-start(bf16[128,12,2048]{2,1,0:T(8,128)(2,1)} %reshape.194), calls=%async_computation.1 | async-start | bytes 16777216 | tf_op jit(solution)/shard_map/all_to_all | solution.py:149
  189.0 157.4 %all-gather.10.cloned.1.call-start = ((), (), s32[]{:S(2)}) async-start(), calls=%async_computation.3 | async-start | bytes 2621440 | tf_op jit(solution)/shard_map/all_gather | solution.py:157
  189.8 156.7 %all-gather.12.cloned.1.call-start = ((), (), s32[]{:S(2)}) async-start(), calls=%async_computation.4 | async-start | bytes 2621440 | tf_op jit(solution)/shard_map/all_gather | solution.py:158
  190.5 185.5 %all-gather.14.cloned.1.call-start = ((), (), s32[]{:S(2)}) async-start(), calls=%async_computation.5 | async-start | bytes 2621440 | tf_op jit(solution)/shard_map/all_gather | solution.py:159
  341.0 3.6 copy-start.5
  345.8 62.7 %all-gather.8.cloned.1.call-start = ((), (), s32[]{:S(2)}) async-start(), calls=%async_computation.2 | async-start | bytes 2621440 | tf_op jit(solution)/shard_map/all_gather | solution.py:160
  346.3 38.9 %copy-start.11 = (s32[16384]{0:T(1024)S(1)}, s32[16384]{0:T(1024)}, u32[]{:S(2)}) copy-start(s32[16384]{0:T(1024)} %param.24) | copy-start | bytes 196612
  346.4 40.2 %copy-start.3 = (bf16[4096,2,128]{2,1,0:T(2,128)(2,1)S(1)}, bf16[4096,2,128]{2,1,0:T(2,128)(2,1)}, u32[]{:S(2)}) copy-start(bf16[4096,2,128]{2,1,0:T(2,128)(2,1)} %param.33) | copy-start | bytes 6291460
  346.4 94.5 %all-gather.16.cloned.1.call-start = ((), (), s32[]{:S(2)}) async-start(), calls=%async_computation.6 | async-start | bytes 2621440 | tf_op jit(solution)/shard_map/all_gather | solution.py:166
  384.9 117.4 %all-gather.18.cloned.1.call-start = ((), (), s32[]{:S(2)}) async-start(), calls=%async_computation.7 | async-start | bytes 8650752 | tf_op jit(solution)/shard_map/all_gather | solution.py:186
  386.6 24.0 %copy-start.13 = (f32[2048]{0:T(1024)S(1)}, f32[2048]{0:T(1024)}, u32[]{:S(2)}) copy-start(f32[2048]{0:T(1024)} %param.30) | copy-start | bytes 24580
  390.8 52.2 %copy-start.14 = (f32[2048]{0:T(1024)S(1)}, f32[2048]{0:T(1024)}, u32[]{:S(2)}) copy-start(f32[2048]{0:T(1024)} %param.31) | copy-start | bytes 24580
  440.8 4.4 copy-start.8
  445.2 1.7 copy-start.6
  445.2 1.6 copy-start.16
  445.2 2.4 copy-start.7
  455.9 5.6 %copy-start.17 = (f32[128]{0:T(128)S(1)}, f32[128]{0:T(128)}, u32[]{:S(2)}) copy-start(f32[128]{0:T(128)} %param.34) | copy-start | bytes 1540
  461.4 1.0 copy-start.9
  461.4 1.0 copy-start.10
  502.4 27.7 %copy-start.1 = (bf16[1,768,2048]{2,1,0:T(8,128)(2,1)S(1)}, bf16[1,768,2048]{2,1,0:T(8,128)(2,1)}, u32[]{:S(2)}) copy-start(bf16[1,768,2048]{2,1,0:T(8,128)(2,1)} %param.28) | copy-start | bytes 9437188
  502.4 1.2 copy-start.2
Sparse Core Ops, SparseCore 0:
  191.5 66.1 all-gather.9
  259.4 53.2 all-gather.11
  345.9 30.1 all-gather.13
  377.6 30.8 all-gather.7
  410.0 30.8 all-gather.15
  450.3 52.0 all-gather.17

commit v2 on v1

v2 whole, which is shorter than its diff:
```python
import jax
import jax.numpy as jnp
from jax import lax
from jax.experimental import pallas as pl
from jax.experimental.pallas import tpu as pltpu
from jax.sharding import PartitionSpec as P

D = 2048
HD = 128
TOPK = 8
SEGS = 4


EPSILON = 1e-06
THETA = 1000000.0
LOG2E = 1.4426950408889634
MESH = pl.DeviceIdType.MESH
N_Z, N_Y, N_CORE, N_X = 4, 4, 2, 4
PEERS = N_Z * N_Y * N_CORE
ROUND = 8
WINDOW = 16
CUTS = 4
CAPACITY = 12
NOWHERE = -1000.0


def offset_of(slot):
    turn = slot // N_CORE
    return ((turn // N_Y + turn) % N_Z, turn % N_Y, slot % N_CORE)


def peer(offset, sign=1):
    here = lax.axis_index("expert")
    z = (here // (N_Y * N_CORE) + sign * offset[0] + N_Z) % N_Z
    y = (here // N_CORE % N_Y + sign * offset[1] + N_Y) % N_Y
    core = (here + offset[2]) % N_CORE
    return (z * N_Y + y) * N_CORE + core


def remote(source, target, sends, arrivals, slot, device):
    return pltpu.make_async_remote_copy(
        src_ref=source,
        dst_ref=target,
        send_sem=sends.at[slot],
        recv_sem=arrivals.at[slot],
        device_id=device,
        device_id_type=MESH,
    )


def greet(devices):
    barrier = pltpu.get_barrier_semaphore()
    for device in devices:
        pl.semaphore_signal(barrier, inc=1, device_id=device, device_id_type=MESH)
    pl.semaphore_wait(barrier, len(devices))


def across(step):
    return (lax.axis_index("expert"), (lax.axis_index("group") + step) % N_X)


def experts_kernel(
    tokens, routing, low, mid, embed, w_gate, w_up, w_down, w_merge, gain,
    merged, embed_rows,
    route, place, weights, shares, all_tokens, packed, arrived, normed, hidden, returned,
    total, partial, halves, high, low_rows, mid_rows, merge_total,
    gate_mat, up_mat, down_mat, merge_mat,
    own, route_sends, route_arrivals, token_sends, token_arrivals, out_sends, out_arrivals,
    back_sends, back_arrivals, tap_sends, tap_arrivals, sum_sends, sum_arrivals,
    high_sends, high_arrivals,
):
    x = lax.axis_index("group")
    rows = tokens.shape[0]
    slots = CAPACITY * N_X
    batch = ROUND * slots
    batches = PEERS // ROUND
    cut = D // CUTS
    steps = range(1, N_X)
    mine = pl.ds(pl.multiple_of(x * rows, rows), rows)

    def columns(part):
        return pl.ds(pl.multiple_of(part * cut, cut), cut)

    def slot_rows(slot):
        return pl.ds(pl.multiple_of(slot * slots, slots), slots)

    def batch_rows(index):
        return pl.ds(pl.multiple_of(index * batch, batch), batch)

    kept = [
        pltpu.make_async_copy(source, target, own.at[index])
        for index, (source, target) in enumerate(
            (
                (routing.at[x], route.at[x]),
                (tokens, all_tokens.at[mine]),
                (w_gate, gate_mat),
                (w_up, up_mat),
                (w_down, down_mat),
                (low, low_rows.at[mine]),
                (mid, mid_rows.at[mine]),
                (w_merge, merge_mat),
                (embed, embed_rows.at[mine]),
            )
        )
    ]
    for copy in kept:
        copy.start()

    barrier = pltpu.get_barrier_semaphore()
    for step in steps:
        pl.semaphore_signal(barrier, inc=1, device_id=across(step), device_id_type=MESH)

    @pl.loop(1, PEERS)
    def _(slot):
        pl.semaphore_signal(
            barrier, inc=1, device_id=(peer(offset_of(slot), -1), x), device_id_type=MESH
        )

    pl.semaphore_wait(barrier, PEERS - 1 + N_X - 1)

    def route_copy(step):
        return remote(
            routing.at[(x + step) % N_X], route.at[x], route_sends, route_arrivals, step - 1,
            across(step),
        )

    def token_copy(part, step):
        return remote(
            tokens.at[:, columns(part)], all_tokens.at[mine, columns(part)],
            token_sends, token_arrivals, (N_X - 1) * part + step - 1, across(step),
        )

    def outward(slot, part):
        return remote(
            packed.at[slot_rows(slot), columns(part)], arrived.at[slot_rows(slot), columns(part)],
            out_sends, out_arrivals, PEERS * part + slot, (peer(offset_of(slot)), x),
        )

    def homeward(slot, part):
        return remote(
            packed.at[slot_rows(slot), columns(part)], returned.at[slot_rows(slot), columns(part)],
            back_sends, back_arrivals, PEERS * part + slot, (peer(offset_of(slot), -1), x),
        )

    def tap_copy(index, step):
        source = (low, mid, embed)[index]
        target = (low_rows, mid_rows, embed_rows)[index]
        return remote(
            source, target.at[mine], tap_sends, tap_arrivals, (N_X - 1) * index + step - 1,
            across(step),
        )

    def sum_copy(part, step):
        theirs = pl.ds(pl.multiple_of((x + step) % N_X * rows, rows), rows)
        return remote(
            partial.at[theirs, columns(part)], halves.at[step - 1, :, columns(part)],
            sum_sends, sum_arrivals, (N_X - 1) * part + step - 1, across(step),
        )

    def high_copy(part, step):
        return remote(
            high.at[mine, columns(part)], high.at[mine, columns(part)],
            high_sends, high_arrivals, (N_X - 1) * part + step - 1, across(step),
        )

    for step in steps:
        route_copy(step).start()
    for part in range(CUTS):
        for step in steps:
            token_copy(part, step).start()
    kept[0].wait()
    for step in steps:
        route_copy(step).wait_recv()

    @pl.loop(0, batches)
    def _(index):
        @pl.loop(0, ROUND)
        def _(inner):
            slot = index * ROUND + inner
            spots = jnp.concatenate(
                [route[block, 0, pl.ds(slot, 1), :] for block in range(N_X)], axis=1
            )
            share = jnp.concatenate(
                [route[block, 1, pl.ds(slot, 1), :] for block in range(N_X)], axis=1
            )
            lines = lax.broadcasted_iota(jnp.int32, (slots, N_X * rows), 0).astype(jnp.float32)
            match = lines == spots
            place[slot_rows(slot), :] = jnp.where(match, 1.0, 0.0).astype(jnp.bfloat16)
            weights[slot_rows(inner), :] = jnp.where(match, share, 0.0)

        shares[:, batch_rows(index)] = weights[...].T.astype(jnp.bfloat16)

    kept[1].wait()

    @pl.loop(0, CUTS)
    def _(part):
        for step in steps:
            token_copy(part, step).wait_recv()

        @pl.loop(0, batches)
        def _(index):
            span = batch_rows(index)
            packed[span, columns(part)] = jnp.dot(
                place[span, :], all_tokens[:, columns(part)], preferred_element_type=jnp.float32
            ).astype(jnp.bfloat16)

            @pl.loop(index * ROUND, (index + 1) * ROUND)
            def _(slot):
                pl.when(slot > 0)(lambda: outward(slot, part).start())

        arrived[slot_rows(0), columns(part)] = packed[slot_rows(0), columns(part)]

    for index in range(3):
        for step in steps:
            tap_copy(index, step).start()
    for copy in kept[2:]:
        copy.wait()

    def reply(index, part):
        span = batch_rows(index)
        packed[span, columns(part)] = jnp.dot(
            hidden[span, :], down_mat[:, columns(part)], preferred_element_type=jnp.float32
        ).astype(jnp.bfloat16)

        @pl.loop(index * ROUND, (index + 1) * ROUND)
        def _(slot):
            pl.when(slot > 0)(lambda: homeward(slot, part).start())

        @pl.when(index == 0)
        def _():
            returned[slot_rows(0), columns(part)] = packed[slot_rows(0), columns(part)]

    def each_copy(index, act):
        @pl.loop(0, ROUND * CUTS)
        def _(inner):
            slot = index * ROUND + inner % ROUND
            pl.when(slot > 0)(lambda: act(slot, inner // ROUND))

    @pl.loop(0, batches)
    def _(index):
        each_copy(index, lambda slot, part: outward(slot, part).wait_recv())

        @pl.loop(0, ROUND)
        def _(inner):
            values = arrived[slot_rows(index * ROUND + inner), :].astype(jnp.float32)
            size = lax.rsqrt(jnp.mean(values * values, axis=-1, keepdims=True) + EPSILON)
            normed[slot_rows(inner), :] = (values * size * gain[...]).astype(jnp.bfloat16)

        @pl.loop(0, w_gate.shape[1] // 256)
        def _(tile):
            tiles = pl.ds(pl.multiple_of(tile * 256, 256), 256)
            gate = jnp.dot(normed[...], gate_mat[:, tiles], preferred_element_type=jnp.float32)
            up = jnp.dot(normed[...], up_mat[:, tiles], preferred_element_type=jnp.float32)
            hidden[batch_rows(index), tiles] = (gate / (1.0 + jnp.exp(-gate)) * up).astype(
                jnp.bfloat16
            )

        each_copy(index, lambda slot, part: outward(slot, part).wait_send())
        reply(index, 0)

    @pl.loop(batches, CUTS * batches)
    def _(turn):
        reply(turn % batches, turn // batches)

    for index in range(2):
        for step in steps:
            tap_copy(index, step).wait_recv()
    merge_total[...] = jnp.zeros_like(merge_total)

    def add_merge(source, index, part):
        depth = pl.ds(pl.multiple_of(index * D + part * cut, cut), cut)
        merge_total[...] += jnp.dot(
            source[:, columns(part)], merge_mat[depth, :], preferred_element_type=jnp.float32
        )

    @pl.loop(0, CUTS)
    def _(part):
        add_merge(low_rows, 0, part)
        add_merge(mid_rows, 1, part)

    def add_high(part):
        for step in steps:
            high_copy(part, step).wait_recv()
        add_merge(high, 2, part)

    @pl.loop(0, CUTS)
    def _(part):
        total[...] = jnp.zeros_like(total)

        @pl.loop(0, batches)
        def _(index):
            @pl.loop(index * ROUND, (index + 1) * ROUND)
            def _(slot):
                pl.when(slot > 0)(lambda: homeward(slot, part).wait_recv())

            span = batch_rows(index)
            total[...] += jnp.dot(
                shares[:, span], returned[span, columns(part)], preferred_element_type=jnp.float32
            )

        partial[:, columns(part)] = total[...].astype(jnp.bfloat16)
        for step in steps:
            sum_copy(part, step).start()
        mixed = all_tokens[mine, columns(part)].astype(jnp.float32) + total[mine, :]
        for step in steps:
            sum_copy(part, step).wait_recv()
            mixed += halves[step - 1, :, columns(part)].astype(jnp.float32)
        high[mine, columns(part)] = mixed.astype(jnp.bfloat16)
        for step in steps:
            high_copy(part, step).start()
        pl.when(part > 0)(lambda: add_high(part - 1))

    add_high(CUTS - 1)
    merged[...] = merge_total[...].astype(jnp.bfloat16)

    @pl.loop(0, batches)
    def _(index):
        each_copy(index, lambda slot, part: homeward(slot, part).wait_send())

    for step in steps:
        route_copy(step).wait_send()
        tap_copy(2, step).wait_recv()
        for index in range(3):
            tap_copy(index, step).wait_send()

        @pl.loop(0, CUTS)
        def _(part):
            token_copy(part, step).wait_send()
            sum_copy(part, step).wait_send()
            high_copy(part, step).wait_send()


def experts(tokens, routing, low, mid, embed, w_gate, w_up, w_down, w_merge, gain):
    rows, width, out_width = tokens.shape[0], w_gate.shape[1], w_merge.shape[1]
    everyone = N_X * rows
    slots = CAPACITY * N_X
    hbm = pl.BlockSpec(memory_space=pl.ANY)
    vmem = pl.BlockSpec(memory_space=pltpu.VMEM)
    dma = pltpu.SemaphoreType.DMA

    def half(*shape):
        return pltpu.VMEM(shape, jnp.bfloat16)

    def full(*shape):
        return pltpu.VMEM(shape, jnp.float32)

    few, many = (N_X - 1) * CUTS, PEERS * CUTS
    return pl.pallas_call(
        experts_kernel,
        out_shape=(
            jax.ShapeDtypeStruct((everyone, out_width), jnp.bfloat16),
            jax.ShapeDtypeStruct((everyone, D), jnp.bfloat16),
        ),
        in_specs=[hbm] * 9 + [vmem],
        out_specs=(vmem, hbm),
        scratch_shapes=[
            full(N_X, 2, PEERS, rows),
            half(PEERS * slots, everyone),
            full(ROUND * slots, everyone),
            half(everyone, PEERS * slots),
            half(everyone, D),
            half(PEERS * slots, D),
            half(PEERS * slots, D),
            half(ROUND * slots, D),
            half(PEERS * slots, width),
            half(PEERS * slots, D),
            full(everyone, D // CUTS),
            half(everyone, D),
            half(N_X - 1, rows, D),
            half(everyone, D),
            half(everyone, D),
            half(everyone, D),
            full(everyone, out_width),
            half(D, width),
            half(D, width),
            half(width, D),
            half(3 * D, out_width),
            dma((9,)),
            dma((N_X - 1,)), dma((N_X - 1,)),
            dma((few,)), dma((few,)),
            dma((many,)), dma((many,)),
            dma((many,)), dma((many,)),
            dma((9,)), dma((9,)),
            dma((few,)), dma((few,)),
            dma((few,)), dma((few,)),
        ],
        compiler_params=pltpu.CompilerParams(
            collective_id=2, has_side_effects=True, vmem_limit_bytes=60 << 20
        ),
        cost_estimate=pl.CostEstimate(
            flops=6 * PEERS * slots * D * width, bytes_accessed=40 << 20, transcendentals=0
        ),
        name="experts",
    )(tokens, routing, low, mid, embed, w_gate, w_up, w_down, w_merge, gain)


def rotation(positions):
    half = HD // 2
    freqs = jnp.power(THETA, -jnp.arange(half, dtype=jnp.float32) * 2.0 / HD)
    angles = positions.astype(jnp.float32)[:, None] * freqs[None, :]
    cosine, sine = jnp.cos(angles), jnp.sin(angles)
    return jnp.concatenate([cosine, cosine], axis=1), jnp.concatenate([-sine, sine], axis=1)


def segment_positions(segments):
    labels = jnp.arange(SEGS, dtype=jnp.int32)
    member = (segments[:, None] == labels[None, :]).astype(jnp.int32)
    counts = jnp.sum(member, axis=0)
    starts = jnp.cumsum(counts) - counts
    return jnp.arange(segments.shape[0], dtype=jnp.int32) - jnp.sum(
        member * starts[None, :], axis=1
    )


def draft_kernel(
    merged, embed, w_query, w_kv, embed_gain, merged_gain, q_gain, k_gain, cosine, sine, row_start,
    out,
    pieces, embeds, joined, embed_total, merged_total, squares, query, held, total,
    query_mat, kv_mat,
    x_sends, x_arrivals, z_sends, z_arrivals, y_sends, y_arrivals, core_sends, core_arrivals, own,
):
    rows, cut = merged.shape
    heads = query.shape[0]
    here, x = lax.axis_index("expert"), lax.axis_index("group")
    z, y, core = here // (N_Y * N_CORE), here // N_CORE % N_Y, here % N_CORE
    loads = [
        pltpu.make_async_copy(source, target, own.at[index])
        for index, (source, target) in enumerate(
            ((merged, pieces.at[x]), (embed, embeds), (w_query, query_mat), (w_kv, kv_mat))
        )
    ]
    for load in loads:
        load.start()
    greet(
        [across(step) for step in (1, 2, 3)]
        + [(peer((step, 0, 0)), x) for step in (1, 2, 3)]
        + [(peer((0, step, 0)), x) for step in (1, 2, 3)]
        + [(peer((0, 0, 1)), x)]
    )
    near, far = 1, N_X - 1
    halves = (pl.ds(0, rows // 2), pl.ds(rows // 2, rows // 2))

    def direct(index):
        return remote(
            merged, pieces.at[x], x_sends, x_arrivals, index, across((near, far)[index])
        )

    def onward(index):
        block = (x + (far, near)[index]) % N_X
        span = halves[index]
        return remote(
            pieces.at[block, span], pieces.at[block, span], x_sends, x_arrivals, 2 + index,
            across((near, far)[index]),
        )

    for index in (0, 1):
        direct(index).start()

    def add_part(source, depth, target):
        target[:, : heads * HD] += jnp.dot(
            source, query_mat[depth, :], preferred_element_type=jnp.float32
        )
        target[:, heads * HD :] += jnp.dot(
            source, kv_mat[depth, :], preferred_element_type=jnp.float32
        )

    def columns(part):
        return pl.ds(pl.multiple_of(part * cut, cut), cut)

    embed_total[...] = jnp.zeros_like(embed_total)
    merged_total[...] = jnp.zeros_like(merged_total)
    squares[...] = jnp.zeros_like(squares)
    loads[1].wait()
    chunk = rows // 8

    @pl.loop(0, 8)
    def _(index):
        span = pl.ds(pl.multiple_of(index * chunk, chunk), chunk)
        values = embeds[span, :].astype(jnp.float32)
        size = lax.rsqrt(jnp.mean(values * values, axis=-1, keepdims=True) + EPSILON)
        joined[span, :] = (values * size * embed_gain[...]).astype(jnp.bfloat16)

    for load in (loads[0], loads[2], loads[3]):
        load.wait()

    @pl.loop(0, N_X)
    def _(part):
        add_part(joined[:, columns(part)], columns(part), embed_total)

    def add_piece(block):
        values = pieces[block].astype(jnp.float32)
        squares[...] += jnp.broadcast_to(
            jnp.sum(values * values, axis=-1, keepdims=True), squares.shape
        )
        source = (values * merged_gain[:, columns(block)]).astype(jnp.bfloat16)
        add_part(source, pl.ds(pl.multiple_of(D + block * cut, cut), cut), merged_total)

    for index in (0, 1):
        direct(index).wait_recv()
        onward(index).start()

    @pl.loop(0, N_X)
    def _(turn):
        @pl.when(turn == N_X - 1)
        def _():
            for index in (0, 1):
                onward(index).wait_recv()

        add_piece((x + jnp.where(turn == 3, 2, jnp.where(turn == 2, 3, turn))) % N_X)

    shrink = lax.rsqrt(squares[:, :1] * (1.0 / D) + EPSILON)

    def project(index):
        span = slice(index * HD, (index + 1) * HD)
        return embed_total[:, span] + merged_total[:, span] * shrink

    def turned(values, gain):
        size = lax.rsqrt(jnp.mean(values * values, axis=-1, keepdims=True) + EPSILON)
        values = values * size * gain[...]
        return values * cosine[...] + pltpu.roll(values, HD // 2, 1) * sine[...]

    for index in range(heads):
        query[index] = (turned(project(index), q_gain) * (HD**-0.5 * LOG2E)).astype(jnp.bfloat16)

    def place(plane, row, column):
        return (plane * N_Y + row) * N_CORE + column

    def wanted(plane, row, reader):
        near = (plane == 0) & (row <= reader)
        return near | ((plane == 1) & (z >= 1)) | ((plane == 2) & (z >= 2) & (row >= reader))

    def along_z(plane):
        return remote(
            held.at[place(0, y, core)], held.at[place(plane, y, core)], z_sends, z_arrivals,
            plane - 1,
            (peer((plane, 0, 0)), x),
        )

    def along_y(plane, step):
        slot = place(plane, y, core)
        return remote(
            held.at[slot], held.at[slot], y_sends, y_arrivals, 3 * plane + step - 1,
            (peer((0, step, 0)), x),
        )

    def to_sibling(plane, row):
        slot = place(plane, row, core)
        return remote(
            held.at[slot], held.at[slot], core_sends, core_arrivals, N_Y * plane + row,
            (peer((0, 0, 1)), x),
        )

    def from_sibling(plane, row):
        slot = place(plane, row, 1 - core)
        return remote(
            held.at[slot], held.at[slot], core_sends, core_arrivals, N_Y * plane + row,
            (peer((0, 0, 1)), x),
        )

    def share(plane):
        for step in (1, 2, 3):
            pl.when(wanted(plane, y, (y + step) % N_Y))(along_y(plane, step).start)

    held[place(0, y, core), 0] = turned(project(heads), k_gain).astype(jnp.bfloat16)
    held[place(0, y, core), 1] = project(heads + 1).astype(jnp.bfloat16)
    for plane in (1, 2):
        pl.when(z + plane < N_Z)(along_z(plane).start)
    total[...] = jnp.zeros_like(total)
    share(0)
    to_sibling(0, y).start()

    def add_block(plane, row, column):
        slot = place(plane, row, column)
        first = ((z - plane) * N_Y * N_CORE + row * N_CORE + column) * rows
        key = held[slot, 0]
        value = jnp.concatenate([held[slot, 1], jnp.ones((rows, HD), jnp.bfloat16)], axis=1)
        query_index = here * rows + lax.broadcasted_iota(jnp.int32, (rows, rows), 0)
        key_index = first + lax.broadcasted_iota(jnp.int32, (rows, rows), 1)
        allowed = (key_index <= query_index) & (key_index >= row_start[...])
        for head in range(heads):
            scores = lax.dot_general(
                query[head], key, (((1,), (1,)), ((), ())), preferred_element_type=jnp.float32
            )
            weights = jnp.where(allowed, jnp.exp2(scores), 0.0).astype(jnp.bfloat16)
            total[head] += jnp.dot(weights, value, preferred_element_type=jnp.float32)

    def needed(plane, row, column):
        behind = here - ((z - plane) * N_Y * N_CORE + row * N_CORE + column)
        return wanted(plane, row, y) & (behind >= 0) & (behind <= WINDOW)

    add_block(0, y, core)
    for plane in (1, 2):

        @pl.when(z >= plane)
        def _():
            along_z(plane).wait_recv()
            share(plane)
            pl.when(wanted(plane, y, y))(to_sibling(plane, y).start)

    @pl.loop(1, 3 * N_Y + 1)
    def _(step):
        plane, back = step // N_Y, step % N_Y
        row = (y + N_Y - back) % N_Y

        @pl.when((step < 3 * N_Y) & wanted(plane, row, y))
        def _():
            @pl.when(back > 0)
            def _():
                slot = place(plane, row, core)
                remote(
                    held.at[slot], held.at[slot], y_sends, y_arrivals, 3 * plane + back - 1,
                    (peer((0, 1, 0)), x),
                ).wait_recv()
                to_sibling(plane, row).start()

            pl.when(needed(plane, row, core))(lambda: add_block(plane, row, core))

        plane, back = (step - 1) // N_Y, (step - 1) % N_Y
        row = (y + N_Y - back) % N_Y

        @pl.when(wanted(plane, row, y))
        def _():
            from_sibling(plane, row).wait_recv()
            pl.when(needed(plane, row, 1 - core))(lambda: add_block(plane, row, 1 - core))

    for head in range(heads):
        out[:, head * HD : (head + 1) * HD] = (
            total[head, :, :HD] / total[head, :, HD:]
        ).astype(out.dtype)
    for plane in (1, 2):
        pl.when(z + plane < N_Z)(along_z(plane).wait_send)
    for plane in (0, 1, 2):
        for step in (1, 2, 3):
            pl.when(wanted(plane, y, (y + step) % N_Y))(along_y(plane, step).wait_send)
        for row in range(N_Y):
            pl.when(wanted(plane, row, y))(to_sibling(plane, row).wait_send)
    for index in (0, 1):
        direct(index).wait_send()
        onward(index).wait_send()


def draft(merged, embed, w_query, w_kv, embed_gain, merged_gain, q_gain, k_gain, cosine, sine, row_start):
    rows, cut = merged.shape
    heads = w_query.shape[1] // HD
    wide = w_query.shape[1] + w_kv.shape[1]
    hbm = pl.BlockSpec(memory_space=pl.ANY)
    vmem = pl.BlockSpec(memory_space=pltpu.VMEM)
    dma = pltpu.SemaphoreType.DMA
    return pl.pallas_call(
        draft_kernel,
        out_shape=jax.ShapeDtypeStruct((rows, heads * HD), jnp.bfloat16),
        in_specs=[hbm] * 4 + [vmem] * 7,
        out_specs=vmem,
        scratch_shapes=[
            pltpu.VMEM((N_X, rows, cut), jnp.bfloat16),
            pltpu.VMEM((rows, D), jnp.bfloat16),
            pltpu.VMEM((rows, D), jnp.bfloat16),
            pltpu.VMEM((rows, wide), jnp.float32),
            pltpu.VMEM((rows, wide), jnp.float32),
            pltpu.VMEM((rows, HD), jnp.float32),
            pltpu.VMEM((heads, rows, HD), jnp.bfloat16),
            pltpu.VMEM((3 * N_Y * N_CORE, 2, rows, HD), jnp.bfloat16),
            pltpu.VMEM((heads, rows, 2 * HD), jnp.float32),
            pltpu.VMEM((2 * D, heads * HD), jnp.bfloat16),
            pltpu.VMEM((2 * D, w_kv.shape[1]), jnp.bfloat16),
            dma((4,)), dma((4,)), dma((2,)), dma((2,)), dma((9,)), dma((9,)), dma((12,)), dma((12,)),
            dma((4,)),
        ],
        compiler_params=pltpu.CompilerParams(
            collective_id=3, has_side_effects=True, vmem_limit_bytes=56 << 20
        ),
        name="draft",
    )(
        merged, embed, w_query, w_kv, embed_gain[None, :], merged_gain[None, :], q_gain[None, :],
        k_gain[None, :], cosine, sine, row_start,
    )


def body(
    tokens,
    low_tap,
    mid_tap,
    next_embed,
    expert_ids,
    gate_weights,
    segments,
    moe_gain,
    w_gate,
    w_up,
    w_down,
    merge_weight,
    embed_gain,
    merged_gain,
    w_query,
    w_kv,
    q_gain,
    k_gain,
):
    rows = tokens.shape[0]
    planes = jnp.arange(N_X, dtype=jnp.int32)
    owners = peer(offset_of(jnp.arange(PEERS, dtype=jnp.int32)))[None, :] * N_X + planes[:, None]
    hits = expert_ids[None, None, :, :] == owners[:, :, None, None]
    member = jnp.any(hits, axis=3)
    share = jnp.sum(jnp.where(hits, gate_weights[None, None], 0.0), axis=3)
    order = jnp.arange(rows, dtype=jnp.int32)
    earlier = (order[:, None] < order[None, :]).astype(jnp.bfloat16)
    ranks = jnp.dot(member.astype(jnp.bfloat16), earlier, preferred_element_type=jnp.float32)
    spots = jnp.where(member, ranks + CAPACITY * lax.axis_index("group"), NOWHERE)
    routing = jnp.stack([spots, share], axis=1)
    merged_part, embed_rows = experts(
        tokens, routing, low_tap, mid_tap, next_embed, w_gate[0], w_up[0], w_down[0],
        merge_weight, moe_gain[None, :],
    )
    block_rows = embed_rows.shape[0]
    first = lax.axis_index("expert") * block_rows
    positions = lax.dynamic_slice_in_dim(segment_positions(segments), first, block_rows)
    row_start = (first + jnp.arange(block_rows, dtype=jnp.int32) - positions)[:, None]
    cosine, sine = rotation(positions)
    return draft(
        merged_part, embed_rows, w_query, w_kv.reshape(w_kv.shape[0], -1), embed_gain, merged_gain,
        q_gain, k_gain, cosine, sine, row_start,
    )


def solution(mesh):
    return jax.shard_map(
        body,
        mesh=mesh,
        in_specs=(
            P(("expert", "group"), None),
            P(("expert", "group"), None),
            P(("expert", "group"), None),
            P(("expert", "group"), None),
            P(("expert", "group"), None),
            P(("expert", "group"), None),
            P(),
            P(),
            P(("expert", "group"), None, None),
            P(("expert", "group"), None, None),
            P(("expert", "group"), None, None),
            P(None, "group"),
            P(),
            P(),
            P(None, "group"),
            P(None, None, "group"),
            P(),
            P(),
        ),
        out_specs=P("expert", "group"),
        check_vma=False,
    )
```

time: 539 us -> 281 us (0.52)
  the two profiles are of different devices: /device:TPU:57 before, /device:TPU:66 now
where the time goes in v2:
time: 281 us
  Pallas kernels  269 us (96%)
  other arithmetic  7.15 us (3%)
  local copies, waits for them, and re-layouts  4.32 us (2%)
    pallas_call x1, Pallas kernels, experts(): pl.pallas_call(experts_kernel, out_shape=(jax.ShapeDtypeStruct((everyone,...  186 us
    pallas_call x1, Pallas kernels, draft(): pl.pallas_call(draft_kernel, out_shape=jax.ShapeDtypeStruct((rows, heads...  83.1 us

profile of v2, /device:TPU:66, one launch (start us, length us, event | category | flops | bytes accessed | tf_op | source)
XLA Modules:
  0.0 280.8 jit_solution(18026226481643690779)
XLA Ops:
  0.0 0.0 copy-start
  0.0 1.2 convert_reduce_fusion
  1.3 0.2 reduce-window.8
  1.5 0.9 compare_reduce_fusion
  2.4 0.1 fusion.1
  2.5 0.9 fusion.2
  3.5 0.7 pad_maximum_fusion.2.routing
  4.2 1.1 select_reduce_fusion
  5.2 0.1 add_subtract_fusion
  5.3 0.9 copy.24.row_start
  6.2 1.0 fusion.3
  7.2 1.0 pad_maximum_fusion
  8.2 0.0 copy-done
  8.2 1.6 copy.27
  9.8 186.0 %experts.1 = (bf16[512,512]{1,0:T(8,128)(2,1)}, bf16[512,2048]{1,0:T(8,128)(2,1)}) custom-call(bf16[128,2048]{1,0:T(8,128)(2,1)} %tokens.1, f32[4,2,32,128]{3,2,1,0:T(8,128)} %pad_maximum_fusion.2.routing, bf16[128,2048]{1,0:T(8,128)(2,1)} %low.1, bf16[128,2048]{1,0:T(8,128)(2,1)} %mid.1, bf16[128,2048]{1,0:T(8,128)(2,1)} %embed.1, ...), custom_call_target="tpu_custom_call" | custom-call | flops 14495514624 | bytes 41943040 | tf_op jit(solution)/shard_map/experts/pallas_call | solution.py:348
  195.8 83.1 %draft.1 = bf16[512,512]{1,0:T(8,128)(2,1)} custom-call(bf16[512,512]{1,0:T(8,128)(2,1)} %get-tuple-element.7.merged, bf16[512,2048]{1,0:T(8,128)(2,1)} %get-tuple-element.8.embed, bf16[4096,512]{1,0:T(8,128)(2,1)} %w_query.1, bf16[4096,256]{1,0:T(8,128)(2,1)} %bitcast.23, f32[1,2048]{1,0:T(1,128)} %bitcast.27, f32[1,2048]{1,0:T(1,128)} %bitcast.28, ...), custom_call_target="tpu_custom_call" | custom-call | tf_op jit(solution)/shard_map/draft/pallas_call | solution.py:649
  278.9 1.9 copy.29
  (4 shorter events, 0.1 us)
Async XLA Ops:
  0.0 8.2 %copy-start = (bf16[4096,2,128]{2,1,0:T(2,128)(2,1)S(1)}, bf16[4096,2,128]{2,1,0:T(2,128)(2,1)}, u32[]{:S(2)}) copy-start(bf16[4096,2,128]{2,1,0:T(2,128)(2,1)} %param.33) | copy-start | bytes 6291460

commit v3 on v2

--- a/solution.py
+++ b/solution.py
@@ -1,5 +1,6 @@
 import jax
 import jax.numpy as jnp
+import numpy as np
 from jax import lax
 from jax.experimental import pallas as pl
 from jax.experimental.pallas import tpu as pltpu
@@ -20,6 +21,7 @@
 ROUND = 8
 WINDOW = 16
 CUTS = 4
+HALVES = (0, 1)
 CAPACITY = 12
 NOWHERE = -1000.0
 
@@ -60,9 +62,9 @@
 
 
 def experts_kernel(
-    tokens, routing, low, mid, embed, w_gate, w_up, w_down, w_merge, gain,
-    merged, embed_rows,
-    route, place, weights, shares, all_tokens, packed, arrived, normed, hidden, returned,
+    tokens, choices, low, mid, embed, w_gate, w_up, w_down, w_merge, gain, segments, freqs,
+    merged, embed_rows, cosine, sine, row_start,
+    routing, route, place, weights, shares, all_tokens, packed, arrived, normed, hidden, returned,
     total, partial, halves, high, low_rows, mid_rows, merge_total,
     gate_mat, up_mat, down_mat, merge_mat,
     own, route_sends, route_arrivals, token_sends, token_arrivals, out_sends, out_arrivals,
@@ -91,7 +93,6 @@
         pltpu.make_async_copy(source, target, own.at[index])
         for index, (source, target) in enumerate(
             (
-                (routing.at[x], route.at[x]),
                 (tokens, all_tokens.at[mine]),
                 (w_gate, gate_mat),
                 (w_up, up_mat),
@@ -116,6 +117,24 @@
             barrier, inc=1, device_id=(peer(offset_of(slot), -1), x), device_id_type=MESH
         )
 
+    slot = lax.broadcasted_iota(jnp.int32, (PEERS, 1), 0)
+    owner = (peer(offset_of(slot)) * N_X).astype(jnp.float32)
+    earlier = lax.broadcasted_iota(jnp.int32, (rows, rows), 0) < lax.broadcasted_iota(
+        jnp.int32, (rows, rows), 1
+    )
+    earlier = jnp.where(earlier, 1.0, 0.0).astype(jnp.bfloat16)
+    for plane in range(N_X):
+        member = jnp.zeros((PEERS, rows), jnp.float32)
+        share = jnp.zeros((PEERS, rows), jnp.float32)
+        for choice in range(TOPK):
+            hit = choices[choice : choice + 1, :] == owner + plane
+            member += jnp.where(hit, 1.0, 0.0)
+            share += jnp.where(hit, choices[TOPK + choice : TOPK + choice + 1, :], 0.0)
+        ranks = jnp.dot(member.astype(jnp.bfloat16), earlier, preferred_element_type=jnp.float32)
+        shift = (CAPACITY * x).astype(jnp.float32)
+        routing[plane, 0] = jnp.where(member > 0.0, ranks + shift, NOWHERE)
+        routing[plane, 1] = share
+
     pl.semaphore_wait(barrier, PEERS - 1 + N_X - 1)
 
     def route_copy(step):
@@ -168,29 +187,24 @@
     for part in range(CUTS):
         for step in steps:
             token_copy(part, step).start()
-    kept[0].wait()
+    route[x] = routing[x]
     for step in steps:
         route_copy(step).wait_recv()
 
-    @pl.loop(0, batches)
-    def _(index):
-        @pl.loop(0, ROUND)
-        def _(inner):
-            slot = index * ROUND + inner
-            spots = jnp.concatenate(
-                [route[block, 0, pl.ds(slot, 1), :] for block in range(N_X)], axis=1
-            )
-            share = jnp.concatenate(
-                [route[block, 1, pl.ds(slot, 1), :] for block in range(N_X)], axis=1
-            )
-            lines = lax.broadcasted_iota(jnp.int32, (slots, N_X * rows), 0).astype(jnp.float32)
-            match = lines == spots
-            place[slot_rows(slot), :] = jnp.where(match, 1.0, 0.0).astype(jnp.bfloat16)
-            weights[slot_rows(inner), :] = jnp.where(match, share, 0.0)
-
-        shares[:, batch_rows(index)] = weights[...].T.astype(jnp.bfloat16)
-
-    kept[1].wait()
+    def spread_line(kind, slot):
+        return jnp.concatenate(
+            [route[block, kind, pl.ds(slot, 1), :] for block in range(N_X)], axis=1
+        )
+
+    def match(slot):
+        lines = lax.broadcasted_iota(jnp.int32, (slots, N_X * rows), 0).astype(jnp.float32)
+        return lines == spread_line(0, slot)
+
+    @pl.loop(0, PEERS)
+    def _(slot):
+        place[slot_rows(slot), :] = jnp.where(match(slot), 1.0, 0.0).astype(jnp.bfloat16)
+
+    kept[0].wait()
 
     @pl.loop(0, CUTS)
     def _(part):
@@ -213,7 +227,31 @@
     for index in range(3):
         for step in steps:
             tap_copy(index, step).start()
-    for copy in kept[2:]:
+
+    @pl.loop(0, batches)
+    def _(index):
+        @pl.loop(0, ROUND)
+        def _(inner):
+            slot = index * ROUND + inner
+            weights[slot_rows(inner), :] = jnp.where(match(slot), spread_line(1, slot), 0.0)
+
+        shares[:, batch_rows(index)] = weights[...].T.astype(jnp.bfloat16)
+
+    line = lax.axis_index("expert") * N_X * rows + lax.broadcasted_iota(
+        jnp.int32, (N_X * rows, 1), 0
+    )
+    line = line.astype(jnp.float32)
+    start = jnp.zeros_like(line)
+    for label in range(1, SEGS):
+        below = jnp.where(segments[...] < label, 1.0, 0.0)
+        count = jnp.sum(jnp.sum(below, axis=1, keepdims=True), axis=0, keepdims=True)
+        start = jnp.maximum(start, jnp.where(count <= line, count, 0.0))
+    row_start[...] = start.astype(jnp.int32)
+    angles = (line - start) * freqs[...]
+    signs = jnp.where(lax.broadcasted_iota(jnp.int32, (1, HD), 1) < HD // 2, -1.0, 1.0)
+    cosine[...] = jnp.cos(angles)
+    sine[...] = jnp.sin(angles) * signs
+    for copy in kept[1:]:
         copy.wait()
 
     def reply(index, part):
@@ -330,7 +368,9 @@
             high_copy(part, step).wait_send()
 
 
-def experts(tokens, routing, low, mid, embed, w_gate, w_up, w_down, w_merge, gain):
+def experts(
+    tokens, choices, low, mid, embed, w_gate, w_up, w_down, w_merge, gain, segments, freqs
+):
     rows, width, out_width = tokens.shape[0], w_gate.shape[1], w_merge.shape[1]
     everyone = N_X * rows
     slots = CAPACITY * N_X
@@ -350,10 +390,14 @@
         out_shape=(
             jax.ShapeDtypeStruct((everyone, out_width), jnp.bfloat16),
             jax.ShapeDtypeStruct((everyone, D), jnp.bfloat16),
+            jax.ShapeDtypeStruct((everyone, HD), jnp.float32),
+            jax.ShapeDtypeStruct((everyone, HD), jnp.float32),
+            jax.ShapeDtypeStruct((everyone, 1), jnp.int32),
         ),
-        in_specs=[hbm] * 9 + [vmem],
-        out_specs=(vmem, hbm),
+        in_specs=[hbm, vmem] + [hbm] * 7 + [vmem] * 3,
+        out_specs=(vmem, hbm, vmem, vmem, vmem),
         scratch_shapes=[
+            full(N_X, 2, PEERS, rows),
             full(N_X, 2, PEERS, rows),
             half(PEERS * slots, everyone),
             full(ROUND * slots, everyone),
@@ -391,24 +435,8 @@
             flops=6 * PEERS * slots * D * width, bytes_accessed=40 << 20, transcendentals=0
         ),
         name="experts",
-    )(tokens, routing, low, mid, embed, w_gate, w_up, w_down, w_merge, gain)
-
-
-def rotation(positions):
-    half = HD // 2
-    freqs = jnp.power(THETA, -jnp.arange(half, dtype=jnp.float32) * 2.0 / HD)
-    angles = positions.astype(jnp.float32)[:, None] * freqs[None, :]
-    cosine, sine = jnp.cos(angles), jnp.sin(angles)
-    return jnp.concatenate([cosine, cosine], axis=1), jnp.concatenate([-sine, sine], axis=1)
-
-
-def segment_positions(segments):
-    labels = jnp.arange(SEGS, dtype=jnp.int32)
-    member = (segments[:, None] == labels[None, :]).astype(jnp.int32)
-    counts = jnp.sum(member, axis=0)
-    starts = jnp.cumsum(counts) - counts
-    return jnp.arange(segments.shape[0], dtype=jnp.int32) - jnp.sum(
-        member * starts[None, :], axis=1
+    )(
+        tokens, choices, low, mid, embed, w_gate, w_up, w_down, w_merge, gain, segments, freqs
     )
 
 
@@ -438,23 +466,29 @@
         + [(peer((0, 0, 1)), x)]
     )
     near, far = 1, N_X - 1
-    halves = (pl.ds(0, rows // 2), pl.ds(rows // 2, rows // 2))
-
-    def direct(index):
-        return remote(
-            merged, pieces.at[x], x_sends, x_arrivals, index, across((near, far)[index])
-        )
-
-    def onward(index):
+    size = rows // len(HALVES)
+
+    def span_of(half):
+        return pl.ds(half * size, size)
+
+    def direct(index, half):
+        span = span_of(half)
+        return remote(
+            merged.at[span], pieces.at[x, span], x_sends, x_arrivals, 4 * half + index,
+            across((near, far)[index]),
+        )
+
+    def onward(index, half):
         block = (x + (far, near)[index]) % N_X
-        span = halves[index]
-        return remote(
-            pieces.at[block, span], pieces.at[block, span], x_sends, x_arrivals, 2 + index,
-            across((near, far)[index]),
-        )
-
-    for index in (0, 1):
-        direct(index).start()
+        span = pl.ds(half * size + index * size // 2, size // 2)
+        return remote(
+            pieces.at[block, span], pieces.at[block, span], x_sends, x_arrivals,
+            4 * half + 2 + index, across((near, far)[index]),
+        )
+
+    for half in HALVES:
+        for index in (0, 1):
+            direct(index, half).start()
 
     def add_part(source, depth, target):
         target[:, : heads * HD] += jnp.dot(
@@ -487,40 +521,33 @@
     def _(part):
         add_part(joined[:, columns(part)], columns(part), embed_total)
 
-    def add_piece(block):
-        values = pieces[block].astype(jnp.float32)
-        squares[...] += jnp.broadcast_to(
-            jnp.sum(values * values, axis=-1, keepdims=True), squares.shape
+    def pass_on(half):
+        for index in (0, 1):
+            direct(index, half).wait_recv()
+            onward(index, half).start()
+
+    def add_piece(block, half):
+        span = span_of(half)
+        values = pieces[block, span].astype(jnp.float32)
+        squares[span, :] += jnp.broadcast_to(
+            jnp.sum(values * values, axis=-1, keepdims=True), (size, HD)
         )
         source = (values * merged_gain[:, columns(block)]).astype(jnp.bfloat16)
-        add_part(source, pl.ds(pl.multiple_of(D + block * cut, cut), cut), merged_total)
-
-    for index in (0, 1):
-        direct(index).wait_recv()
-        onward(index).start()
-
-    @pl.loop(0, N_X)
-    def _(turn):
-        @pl.when(turn == N_X - 1)
-        def _():
-            for index in (0, 1):
-                onward(index).wait_recv()
-
-        add_piece((x + jnp.where(turn == 3, 2, jnp.where(turn == 2, 3, turn))) % N_X)
-
-    shrink = lax.rsqrt(squares[:, :1] * (1.0 / D) + EPSILON)
-
-    def project(index):
-        span = slice(index * HD, (index + 1) * HD)
-        return embed_total[:, span] + merged_total[:, span] * shrink
-
-    def turned(values, gain):
-        size = lax.rsqrt(jnp.mean(values * values, axis=-1, keepdims=True) + EPSILON)
-        values = values * size * gain[...]
-        return values * cosine[...] + pltpu.roll(values, HD // 2, 1) * sine[...]
-
-    for index in range(heads):
-        query[index] = (turned(project(index), q_gain) * (HD**-0.5 * LOG2E)).astype(jnp.bfloat16)
+        joined[span, columns(block)] = source
+        depth = pl.ds(pl.multiple_of(D + block * cut, cut), cut)
+        merged_total[span, heads * HD :] += jnp.dot(
+            source, kv_mat[depth, :], preferred_element_type=jnp.float32
+        )
+
+    def project(index, span):
+        shrink = lax.rsqrt(squares[span, :1] * (1.0 / D) + EPSILON)
+        lanes = slice(index * HD, (index + 1) * HD)
+        return embed_total[span, lanes] + merged_total[span, lanes] * shrink
+
+    def turned(values, gain, span):
+        scale = lax.rsqrt(jnp.mean(values * values, axis=-1, keepdims=True) + EPSILON)
+        values = values * scale * gain[...]
+        return values * cosine[span, :] + pltpu.roll(values, HD // 2, 1) * sine[span, :]
 
     def place(plane, row, column):
         return (plane * N_Y + row) * N_CORE + column
@@ -529,45 +556,69 @@
         near = (plane == 0) & (row <= reader)
         return near | ((plane == 1) & (z >= 1)) | ((plane == 2) & (z >= 2) & (row >= reader))
 
-    def along_z(plane):
-        return remote(
-            held.at[place(0, y, core)], held.at[place(plane, y, core)], z_sends, z_arrivals,
-            plane - 1,
-            (peer((plane, 0, 0)), x),
-        )
-
-    def along_y(plane, step):
-        slot = place(plane, y, core)
-        return remote(
-            held.at[slot], held.at[slot], y_sends, y_arrivals, 3 * plane + step - 1,
+    def along_z(plane, half):
+        span = span_of(half)
+        return remote(
+            held.at[place(0, y, core), :, span], held.at[place(plane, y, core), :, span],
+            z_sends, z_arrivals, 2 * (plane - 1) + half, (peer((plane, 0, 0)), x),
+        )
+
+    def along_y(plane, step, half):
+        part = held.at[place(plane, y, core), :, span_of(half)]
+        return remote(
+            part, part, y_sends, y_arrivals, 2 * (3 * plane + step - 1) + half,
             (peer((0, step, 0)), x),
         )
 
-    def to_sibling(plane, row):
-        slot = place(plane, row, core)
-        return remote(
-            held.at[slot], held.at[slot], core_sends, core_arrivals, N_Y * plane + row,
+    def from_y(plane, step, row, half):
+        part = held.at[place(plane, row, core), :, span_of(half)]
+        return remote(
+            part, part, y_sends, y_arrivals, 2 * (3 * plane + step - 1) + half,
+            (peer((0, 1, 0)), x),
+        )
+
+    def sibling(plane, row, column, half):
+        part = held.at[place(plane, row, column), :, span_of(half)]
+        return remote(
+            part, part, core_sends, core_arrivals, 2 * (N_Y * plane + row) + half,
             (peer((0, 0, 1)), x),
         )
 
-    def from_sibling(plane, row):
-        slot = place(plane, row, 1 - core)
-        return remote(
-            held.at[slot], held.at[slot], core_sends, core_arrivals, N_Y * plane + row,
-            (peer((0, 0, 1)), x),
-        )
-
-    def share(plane):
+    def share(plane, half):
         for step in (1, 2, 3):
-            pl.when(wanted(plane, y, (y + step) % N_Y))(along_y(plane, step).start)
-
-    held[place(0, y, core), 0] = turned(project(heads), k_gain).astype(jnp.bfloat16)
-    held[place(0, y, core), 1] = project(heads + 1).astype(jnp.bfloat16)
-    for plane in (1, 2):
-        pl.when(z + plane < N_Z)(along_z(plane).start)
+            pl.when(wanted(plane, y, (y + step) % N_Y))(along_y(plane, step, half).start)
+
     total[...] = jnp.zeros_like(total)
-    share(0)
-    to_sibling(0, y).start()
+    pass_on(0)
+    for half in HALVES:
+        for turn in (0, 3, 1):
+            add_piece((x + turn) % N_X, half)
+        if half == 0:
+            pass_on(1)
+        for index in (0, 1):
+            onward(index, half).wait_recv()
+        add_piece((x + 2) % N_X, half)
+        span = span_of(half)
+        mine = place(0, y, core)
+        held[mine, 0, span] = turned(project(heads, span), k_gain, span).astype(jnp.bfloat16)
+        held[mine, 1, span] = project(heads + 1, span).astype(jnp.bfloat16)
+        for plane in (2, 1):
+            pl.when(z + plane < N_Z)(along_z(plane, half).start)
+        share(0, half)
+        sibling(0, y, core, half).start()
+
+    @pl.loop(0, N_X)
+    def _(part):
+        depth = pl.ds(pl.multiple_of(D + part * cut, cut), cut)
+        merged_total[:, : heads * HD] += jnp.dot(
+            joined[:, columns(part)], query_mat[depth, :], preferred_element_type=jnp.float32
+        )
+
+    everything = pl.ds(0, rows)
+    for index in range(heads):
+        query[index] = (
+            turned(project(index, everything), q_gain, everything) * (HD**-0.5 * LOG2E)
+        ).astype(jnp.bfloat16)
 
     def add_block(plane, row, column):
         slot = place(plane, row, column)
@@ -588,14 +639,18 @@
         behind = here - ((z - plane) * N_Y * N_CORE + row * N_CORE + column)
         return wanted(plane, row, y) & (behind >= 0) & (behind <= WINDOW)
 
-    add_block(0, y, core)
-    for plane in (1, 2):
-
+    def pass_plane(plane, half):
         @pl.when(z >= plane)
         def _():
-            along_z(plane).wait_recv()
-            share(plane)
-            pl.when(wanted(plane, y, y))(to_sibling(plane, y).start)
+            along_z(plane, half).wait_recv()
+            share(plane, half)
+            pl.when(wanted(plane, y, y))(sibling(plane, y, core, half).start)
+
+    for half in HALVES:
+        pass_plane(1, half)
+    add_block(0, y, core)
+    for half in HALVES:
+        pass_plane(2, half)
 
     @pl.loop(1, 3 * N_Y + 1)
     def _(step):
@@ -606,12 +661,9 @@
         def _():
             @pl.when(back > 0)
             def _():
-                slot = place(plane, row, core)
-                remote(
-                    held.at[slot], held.at[slot], y_sends, y_arrivals, 3 * plane + back - 1,
-                    (peer((0, 1, 0)), x),
-                ).wait_recv()
-                to_sibling(plane, row).start()
+                for half in HALVES:
+                    from_y(plane, back, row, half).wait_recv()
+                    sibling(plane, row, core, half).start()
 
             pl.when(needed(plane, row, core))(lambda: add_block(plane, row, core))
 
@@ -620,23 +672,25 @@
 
         @pl.when(wanted(plane, row, y))
         def _():
-            from_sibling(plane, row).wait_recv()
+            for half in HALVES:
+                sibling(plane, row, 1 - core, half).wait_recv()
             pl.when(needed(plane, row, 1 - core))(lambda: add_block(plane, row, 1 - core))
 
     for head in range(heads):
         out[:, head * HD : (head + 1) * HD] = (
             total[head, :, :HD] / total[head, :, HD:]
         ).astype(out.dtype)
-    for plane in (1, 2):
-        pl.when(z + plane < N_Z)(along_z(plane).wait_send)
-    for plane in (0, 1, 2):
-        for step in (1, 2, 3):
-            pl.when(wanted(plane, y, (y + step) % N_Y))(along_y(plane, step).wait_send)
-        for row in range(N_Y):
-            pl.when(wanted(plane, row, y))(to_sibling(plane, row).wait_send)
-    for index in (0, 1):
-        direct(index).wait_send()
-        onward(index).wait_send()
+    for half in HALVES:
+        for plane in (1, 2):
+            pl.when(z + plane < N_Z)(along_z(plane, half).wait_send)
+        for plane in (0, 1, 2):
+            for step in (1, 2, 3):
+                pl.when(wanted(plane, y, (y + step) % N_Y))(along_y(plane, step, half).wait_send)
+            for row in range(N_Y):
+                pl.when(wanted(plane, row, y))(sibling(plane, row, core, half).wait_send)
+        for index in (0, 1):
+            direct(index, half).wait_send()
+            onward(index, half).wait_send()
 
 
 def draft(merged, embed, w_query, w_kv, embed_gain, merged_gain, q_gain, k_gain, cosine, sine, row_start):
@@ -663,7 +717,7 @@
             pltpu.VMEM((heads, rows, 2 * HD), jnp.float32),
             pltpu.VMEM((2 * D, heads * HD), jnp.bfloat16),
             pltpu.VMEM((2 * D, w_kv.shape[1]), jnp.bfloat16),
-            dma((4,)), dma((4,)), dma((2,)), dma((2,)), dma((9,)), dma((9,)), dma((12,)), dma((12,)),
+            dma((8,)), dma((8,)), dma((4,)), dma((4,)), dma((18,)), dma((18,)), dma((24,)), dma((24,)),
             dma((4,)),
         ],
         compiler_params=pltpu.CompilerParams(
@@ -696,28 +750,16 @@
     q_gain,
     k_gain,
 ):
-    rows = tokens.shape[0]
-    planes = jnp.arange(N_X, dtype=jnp.int32)
-    owners = peer(offset_of(jnp.arange(PEERS, dtype=jnp.int32)))[None, :] * N_X + planes[:, None]
-    hits = expert_ids[None, None, :, :] == owners[:, :, None, None]
-    member = jnp.any(hits, axis=3)
-    share = jnp.sum(jnp.where(hits, gate_weights[None, None], 0.0), axis=3)
-    order = jnp.arange(rows, dtype=jnp.int32)
-    earlier = (order[:, None] < order[None, :]).astype(jnp.bfloat16)
-    ranks = jnp.dot(member.astype(jnp.bfloat16), earlier, preferred_element_type=jnp.float32)
-    spots = jnp.where(member, ranks + CAPACITY * lax.axis_index("group"), NOWHERE)
-    routing = jnp.stack([spots, share], axis=1)
-    merged_part, embed_rows = experts(
-        tokens, routing, low_tap, mid_tap, next_embed, w_gate[0], w_up[0], w_down[0],
-        merge_weight, moe_gain[None, :],
-    )
-    block_rows = embed_rows.shape[0]
-    first = lax.axis_index("expert") * block_rows
-    positions = lax.dynamic_slice_in_dim(segment_positions(segments), first, block_rows)
-    row_start = (first + jnp.arange(block_rows, dtype=jnp.int32) - positions)[:, None]
-    cosine, sine = rotation(positions)
+    choices = jnp.concatenate([expert_ids.astype(jnp.float32), gate_weights], axis=1).T
+    half = HD // 2
+    freqs = np.power(THETA, -np.arange(half) * 2.0 / HD).astype(np.float32)
+    freqs = np.concatenate([freqs, freqs])[None, :]
+    merged, embed_rows, cosine, sine, row_start = experts(
+        tokens, choices, low_tap, mid_tap, next_embed, w_gate[0], w_up[0], w_down[0],
+        merge_weight, moe_gain[None, :], segments.reshape(-1, HD), jnp.asarray(freqs),
+    )
     return draft(
-        merged_part, embed_rows, w_query, w_kv.reshape(w_kv.shape[0], -1), embed_gain, merged_gain,
+        merged, embed_rows, w_query, w_kv.reshape(w_kv.shape[0], -1), embed_gain, merged_gain,
         q_gain, k_gain, cosine, sine, row_start,
     )
 

time: 281 us -> 275 us (0.979)
  other arithmetic: 7.15 us -> 1.97 us
  Pallas kernels: 269 us -> 266 us
    pallas_call x1, Pallas kernels: 83.1 us -> 79.2 us  [draft(): pl.pallas_call(draft_kernel, out_shape=jax.ShapeDtypeStruct((rows, heads...]
    reduce_sum x3 -> x0, other arithmetic: 3.25 us -> none  [the longest x1 1.23 us: segment_positions(): counts = jnp.sum(member, axis=0)]
where the time goes in v3:
time: 275 us; the launch traced here: 273 us
  Pallas kernels  266 us (97%)
  local copies, waits for them, and re-layouts  5.04 us (2%)
    pallas_call x1, Pallas kernels, experts(): pl.pallas_call(experts_kernel, out_shape=(jax.ShapeDtypeStruct((everyone,...  187 us
    pallas_call x1, Pallas kernels, draft(): pl.pallas_call(draft_kernel, out_shape=jax.ShapeDtypeStruct((rows, heads...  79.2 us

profile of v3, /device:TPU:66, one launch (start us, length us, event | category | flops | bytes accessed | tf_op | source)
XLA Modules:
  0.0 272.9 jit_solution(9753906146784290928)
XLA Ops:
  0.0 0.7 convert_element_type.3
  0.7 1.3 maximum_bitcast_fusion.choices
  2.0 3.2 %copy.22 = bf16[512,8,2,128]{3,1,2,0:T(8,128)(2,1)} copy(bf16[512,8,2,128]{3,2,1,0:T(2,128)(2,1)} %bitcast.16) | data formatting | bytes 4194304
  5.1 186.6 %experts.1 = (bf16[512,512]{1,0:T(8,128)(2,1)}, bf16[512,2048]{1,0:T(8,128)(2,1)}, f32[512,128]{1,0:T(8,128)}, f32[512,128]{1,0:T(8,128)}, s32[512,1]{1,0:T(8,128)}) custom-call(bf16[128,2048]{1,0:T(8,128)(2,1)} %tokens.1, f32[16,128]{1,0:T(8,128)} %maximum_bitcast_fusion.choices, bf16[128,2048]{1,0:T(8,128)(2,1)} %low.1, bf16[128,2048]{1,0:T(8,128)(2,1)} %mid.1, ...), custom_call_target="tpu_custom_call" | custom-call | flops 14495514624 | bytes 41943040 | tf_op jit(solution)/shard_map/experts/pallas_call | solution.py:388
  191.8 79.2 %draft.1 = bf16[512,512]{1,0:T(8,128)(2,1)} custom-call(bf16[512,512]{1,0:T(8,128)(2,1)} %get-tuple-element.10.merged, bf16[512,2048]{1,0:T(8,128)(2,1)} %get-tuple-element.11.embed, bf16[4096,512]{1,0:T(8,128)(2,1)} %w_query.1, bf16[4096,256]{1,0:T(8,128)(2,1)} %bitcast.15, f32[1,2048]{1,0:T(1,128)} %bitcast.17, f32[1,2048]{1,0:T(1,128)} %bitcast.18, ...), custom_call_target="tpu_custom_call" | custom-call | tf_op jit(solution)/shard_map/draft/pallas_call | solution.py:703
  271.0 1.9 copy.24

commit v4 on v3

--- a/solution.py
+++ b/solution.py
@@ -62,7 +62,7 @@
 
 
 def experts_kernel(
-    tokens, choices, low, mid, embed, w_gate, w_up, w_down, w_merge, gain, segments, freqs,
+    tokens, choices, gates, low, mid, embed, w_gate, w_up, w_down, w_merge, gain, segments, freqs,
     merged, embed_rows, cosine, sine, row_start,
     routing, route, place, weights, shares, all_tokens, packed, arrived, normed, hidden, returned,
     total, partial, halves, high, low_rows, mid_rows, merge_total,
@@ -118,7 +118,7 @@
         )
 
     slot = lax.broadcasted_iota(jnp.int32, (PEERS, 1), 0)
-    owner = (peer(offset_of(slot)) * N_X).astype(jnp.float32)
+    owner = peer(offset_of(slot)) * N_X
     earlier = lax.broadcasted_iota(jnp.int32, (rows, rows), 0) < lax.broadcasted_iota(
         jnp.int32, (rows, rows), 1
     )
@@ -129,7 +129,7 @@
         for choice in range(TOPK):
             hit = choices[choice : choice + 1, :] == owner + plane
             member += jnp.where(hit, 1.0, 0.0)
-            share += jnp.where(hit, choices[TOPK + choice : TOPK + choice + 1, :], 0.0)
+            share += jnp.where(hit, gates[choice : choice + 1, :], 0.0)
         ranks = jnp.dot(member.astype(jnp.bfloat16), earlier, preferred_element_type=jnp.float32)
         shift = (CAPACITY * x).astype(jnp.float32)
         routing[plane, 0] = jnp.where(member > 0.0, ranks + shift, NOWHERE)
@@ -184,7 +184,7 @@
 
     for step in steps:
         route_copy(step).start()
-    for part in range(CUTS):
+    for part in range(2):
         for step in steps:
             token_copy(part, step).start()
     route[x] = routing[x]
@@ -210,6 +210,11 @@
     def _(part):
         for step in steps:
             token_copy(part, step).wait_recv()
+
+        @pl.when(part + 2 < CUTS)
+        def _():
+            for step in steps:
+                token_copy(part + 2, step).start()
 
         @pl.loop(0, batches)
         def _(index):
@@ -369,7 +374,7 @@
 
 
 def experts(
-    tokens, choices, low, mid, embed, w_gate, w_up, w_down, w_merge, gain, segments, freqs
+    tokens, choices, gates, low, mid, embed, w_gate, w_up, w_down, w_merge, gain, segments, freqs
 ):
     rows, width, out_width = tokens.shape[0], w_gate.shape[1], w_merge.shape[1]
     everyone = N_X * rows
@@ -394,7 +399,7 @@
             jax.ShapeDtypeStruct((everyone, HD), jnp.float32),
             jax.ShapeDtypeStruct((everyone, 1), jnp.int32),
         ),
-        in_specs=[hbm, vmem] + [hbm] * 7 + [vmem] * 3,
+        in_specs=[hbm, vmem, vmem] + [hbm] * 7 + [vmem] * 3,
         out_specs=(vmem, hbm, vmem, vmem, vmem),
         scratch_shapes=[
             full(N_X, 2, PEERS, rows),
@@ -436,7 +441,7 @@
         ),
         name="experts",
     )(
-        tokens, choices, low, mid, embed, w_gate, w_up, w_down, w_merge, gain, segments, freqs
+        tokens, choices, gates, low, mid, embed, w_gate, w_up, w_down, w_merge, gain, segments, freqs
     )
 
 
@@ -486,9 +491,8 @@
             4 * half + 2 + index, across((near, far)[index]),
         )
 
-    for half in HALVES:
-        for index in (0, 1):
-            direct(index, half).start()
+    for index in (0, 1):
+        direct(index, 0).start()
 
     def add_part(source, depth, target):
         target[:, : heads * HD] += jnp.dot(
@@ -514,17 +518,16 @@
         size = lax.rsqrt(jnp.mean(values * values, axis=-1, keepdims=True) + EPSILON)
         joined[span, :] = (values * size * embed_gain[...]).astype(jnp.bfloat16)
 
+    for index in (0, 1):
+        direct(index, 0).wait_recv()
+        onward(index, 0).start()
+        direct(index, 1).start()
     for load in (loads[0], loads[2], loads[3]):
         load.wait()
 
     @pl.loop(0, N_X)
     def _(part):
         add_part(joined[:, columns(part)], columns(part), embed_total)
-
-    def pass_on(half):
-        for index in (0, 1):
-            direct(index, half).wait_recv()
-            onward(index, half).start()
 
     def add_piece(block, half):
         span = span_of(half)
@@ -589,12 +592,13 @@
             pl.when(wanted(plane, y, (y + step) % N_Y))(along_y(plane, step, half).start)
 
     total[...] = jnp.zeros_like(total)
-    pass_on(0)
     for half in HALVES:
         for turn in (0, 3, 1):
             add_piece((x + turn) % N_X, half)
         if half == 0:
-            pass_on(1)
+            for index in (0, 1):
+                direct(index, 1).wait_recv()
+                onward(index, 1).start()
         for index in (0, 1):
             onward(index, half).wait_recv()
         add_piece((x + 2) % N_X, half)
@@ -606,6 +610,15 @@
             pl.when(z + plane < N_Z)(along_z(plane, half).start)
         share(0, half)
         sibling(0, y, core, half).start()
+
+    def pass_plane(plane, half):
+        @pl.when(z >= plane)
+        def _():
+            along_z(plane, half).wait_recv()
+            share(plane, half)
+            pl.when(wanted(plane, y, y))(sibling(plane, y, core, half).start)
+
+    pass_plane(1, 0)
 
     @pl.loop(0, N_X)
     def _(part):
@@ -639,15 +652,7 @@
         behind = here - ((z - plane) * N_Y * N_CORE + row * N_CORE + column)
         return wanted(plane, row, y) & (behind >= 0) & (behind <= WINDOW)
 
-    def pass_plane(plane, half):
-        @pl.when(z >= plane)
-        def _():
-            along_z(plane, half).wait_recv()
-            share(plane, half)
-            pl.when(wanted(plane, y, y))(sibling(plane, y, core, half).start)
-
-    for half in HALVES:
-        pass_plane(1, half)
+    pass_plane(1, 1)
     add_block(0, y, core)
     for half in HALVES:
         pass_plane(2, half)
@@ -750,13 +755,12 @@
     q_gain,
     k_gain,
 ):
-    choices = jnp.concatenate([expert_ids.astype(jnp.float32), gate_weights], axis=1).T
     half = HD // 2
     freqs = np.power(THETA, -np.arange(half) * 2.0 / HD).astype(np.float32)
     freqs = np.concatenate([freqs, freqs])[None, :]
     merged, embed_rows, cosine, sine, row_start = experts(
-        tokens, choices, low_tap, mid_tap, next_embed, w_gate[0], w_up[0], w_down[0],
-        merge_weight, moe_gain[None, :], segments.reshape(-1, HD), jnp.asarray(freqs),
+        tokens, expert_ids.T, gate_weights.T, low_tap, mid_tap, next_embed, w_gate[0], w_up[0],
+        w_down[0], merge_weight, moe_gain[None, :], segments.reshape(-1, HD), jnp.asarray(freqs),
     )
     return draft(
         merged, embed_rows, w_query, w_kv.reshape(w_kv.shape[0], -1), embed_gain, merged_gain,

time: 275 us -> 270 us (0.982)
  no operation moved by 1% of the time
where the time goes in v4:
time: 270 us
  Pallas kernels  265 us (98%)
  local copies, waits for them, and re-layouts  5.04 us (2%)
    pallas_call x1, Pallas kernels, experts(): pl.pallas_call(experts_kernel, out_shape=(jax.ShapeDtypeStruct((everyone,...  186 us
    pallas_call x1, Pallas kernels, draft(): pl.pallas_call(draft_kernel, out_shape=jax.ShapeDtypeStruct((rows, heads...  78.6 us

profile of v4, /device:TPU:66, one launch (start us, length us, event | category | flops | bytes accessed | tf_op | source)
XLA Modules:
  0.0 270.0 jit_solution(8587102311980617457)
XLA Ops:
  0.0 3.2 %copy.22 = bf16[512,8,2,128]{3,1,2,0:T(8,128)(2,1)} copy(bf16[512,8,2,128]{3,2,1,0:T(2,128)(2,1)} %bitcast.16) | data formatting | bytes 4194304
  3.2 186.3 %experts.1 = (bf16[512,512]{1,0:T(8,128)(2,1)}, bf16[512,2048]{1,0:T(8,128)(2,1)}, f32[512,128]{1,0:T(8,128)}, f32[512,128]{1,0:T(8,128)}, s32[512,1]{1,0:T(8,128)}) custom-call(bf16[128,2048]{1,0:T(8,128)(2,1)} %tokens.1, s32[8,128]{1,0:T(8,128)} %bitcast.26, f32[8,128]{1,0:T(8,128)} %bitcast.27, bf16[128,2048]{1,0:T(8,128)(2,1)} %low.1, ...), custom_call_target="tpu_custom_call" | custom-call | flops 14495514624 | bytes 41943040 | tf_op jit(solution)/shard_map/experts/pallas_call | solution.py:393
  189.5 78.6 %draft.1 = bf16[512,512]{1,0:T(8,128)(2,1)} custom-call(bf16[512,512]{1,0:T(8,128)(2,1)} %get-tuple-element.10.merged, bf16[512,2048]{1,0:T(8,128)(2,1)} %get-tuple-element.11.embed, bf16[4096,512]{1,0:T(8,128)(2,1)} %w_query.1, bf16[4096,256]{1,0:T(8,128)(2,1)} %bitcast.15, f32[1,2048]{1,0:T(1,128)} %bitcast.17, f32[1,2048]{1,0:T(1,128)} %bitcast.18, ...), custom_call_target="tpu_custom_call" | custom-call | tf_op jit(solution)/shard_map/draft/pallas_call | solution.py:708
  268.1 1.9 copy.24

commit v5 on v4

--- a/solution.py
+++ b/solution.py
@@ -654,11 +654,13 @@
 
     pass_plane(1, 1)
     add_block(0, y, core)
-    for half in HALVES:
-        pass_plane(2, half)
-
     @pl.loop(1, 3 * N_Y + 1)
     def _(step):
+        @pl.when(step == jnp.where(y == 0, 2 * N_Y, N_Y))
+        def _():
+            for half in HALVES:
+                pass_plane(2, half)
+
         plane, back = step // N_Y, step % N_Y
         row = (y + N_Y - back) % N_Y
 

time: 270 us -> 264 us (0.978)
  Pallas kernels: 265 us -> 259 us
    pallas_call x1, Pallas kernels: 78.6 us -> 72.9 us  [draft(): pl.pallas_call(draft_kernel, out_shape=jax.ShapeDtypeStruct((rows, heads...]
where the time goes in v5:
time: 264 us
  Pallas kernels  259 us (98%)
  local copies, waits for them, and re-layouts  5.04 us (2%)
    pallas_call x1, Pallas kernels, experts(): pl.pallas_call(experts_kernel, out_shape=(jax.ShapeDtypeStruct((everyone,...  186 us
    pallas_call x1, Pallas kernels, draft(): pl.pallas_call(draft_kernel, out_shape=jax.ShapeDtypeStruct((rows, heads...  72.9 us

profile of v5, /device:TPU:66, one launch (start us, length us, event | category | flops | bytes accessed | tf_op | source)
XLA Modules:
  0.0 264.2 jit_solution(18247659309413804383)
XLA Ops:
  0.0 3.2 %copy.22 = bf16[512,8,2,128]{3,1,2,0:T(8,128)(2,1)} copy(bf16[512,8,2,128]{3,2,1,0:T(2,128)(2,1)} %bitcast.16) | data formatting | bytes 4194304
  3.2 186.3 %experts.1 = (bf16[512,512]{1,0:T(8,128)(2,1)}, bf16[512,2048]{1,0:T(8,128)(2,1)}, f32[512,128]{1,0:T(8,128)}, f32[512,128]{1,0:T(8,128)}, s32[512,1]{1,0:T(8,128)}) custom-call(bf16[128,2048]{1,0:T(8,128)(2,1)} %tokens.1, s32[8,128]{1,0:T(8,128)} %bitcast.26, f32[8,128]{1,0:T(8,128)} %bitcast.27, bf16[128,2048]{1,0:T(8,128)(2,1)} %low.1, ...), custom_call_target="tpu_custom_call" | custom-call | flops 14495514624 | bytes 41943040 | tf_op jit(solution)/shard_map/experts/pallas_call | solution.py:393
  189.5 72.9 %draft.1 = bf16[512,512]{1,0:T(8,128)(2,1)} custom-call(bf16[512,512]{1,0:T(8,128)(2,1)} %get-tuple-element.10.merged, bf16[512,2048]{1,0:T(8,128)(2,1)} %get-tuple-element.11.embed, bf16[4096,512]{1,0:T(8,128)(2,1)} %w_query.1, bf16[4096,256]{1,0:T(8,128)(2,1)} %bitcast.15, f32[1,2048]{1,0:T(1,128)} %bitcast.17, f32[1,2048]{1,0:T(1,128)} %bitcast.18, ...), custom_call_target="tpu_custom_call" | custom-call | tf_op jit(solution)/shard_map/draft/pallas_call | solution.py:710
  262.4 1.9 copy.24

commit v6 on v5

--- a/solution.py
+++ b/solution.py
@@ -656,7 +656,7 @@
     add_block(0, y, core)
     @pl.loop(1, 3 * N_Y + 1)
     def _(step):
-        @pl.when(step == jnp.where(y == 0, 2 * N_Y, N_Y))
+        @pl.when(step == jnp.where(y == 0, 2 * N_Y, N_Y - 1))
         def _():
             for half in HALVES:
                 pass_plane(2, half)

time: 264 us -> 262 us (level)
  no operation moved by 1% of the time
where the time goes in v6:
time: 262 us
  Pallas kernels  257 us (98%)
  local copies, waits for them, and re-layouts  5.04 us (2%)
    pallas_call x1, Pallas kernels, experts(): pl.pallas_call(experts_kernel, out_shape=(jax.ShapeDtypeStruct((everyone,...  186 us
    pallas_call x1, Pallas kernels, draft(): pl.pallas_call(draft_kernel, out_shape=jax.ShapeDtypeStruct((rows, heads...  70.8 us

profile of v6, /device:TPU:66, one launch (start us, length us, event | category | flops | bytes accessed | tf_op | source)
XLA Modules:
  0.0 262.2 jit_solution(15644824372121157127)
XLA Ops:
  0.0 3.2 %copy.22 = bf16[512,8,2,128]{3,1,2,0:T(8,128)(2,1)} copy(bf16[512,8,2,128]{3,2,1,0:T(2,128)(2,1)} %bitcast.16) | data formatting | bytes 4194304
  3.2 186.3 %experts.1 = (bf16[512,512]{1,0:T(8,128)(2,1)}, bf16[512,2048]{1,0:T(8,128)(2,1)}, f32[512,128]{1,0:T(8,128)}, f32[512,128]{1,0:T(8,128)}, s32[512,1]{1,0:T(8,128)}) custom-call(bf16[128,2048]{1,0:T(8,128)(2,1)} %tokens.1, s32[8,128]{1,0:T(8,128)} %bitcast.26, f32[8,128]{1,0:T(8,128)} %bitcast.27, bf16[128,2048]{1,0:T(8,128)(2,1)} %low.1, ...), custom_call_target="tpu_custom_call" | custom-call | flops 14495514624 | bytes 41943040 | tf_op jit(solution)/shard_map/experts/pallas_call | solution.py:393
  189.5 70.8 %draft.1 = bf16[512,512]{1,0:T(8,128)(2,1)} custom-call(bf16[512,512]{1,0:T(8,128)(2,1)} %get-tuple-element.10.merged, bf16[512,2048]{1,0:T(8,128)(2,1)} %get-tuple-element.11.embed, bf16[4096,512]{1,0:T(8,128)(2,1)} %w_query.1, bf16[4096,256]{1,0:T(8,128)(2,1)} %bitcast.15, f32[1,2048]{1,0:T(1,128)} %bitcast.17, f32[1,2048]{1,0:T(1,128)} %bitcast.18, ...), custom_call_target="tpu_custom_call" | custom-call | tf_op jit(solution)/shard_map/draft/pallas_call | solution.py:710
  260.3 1.9 copy.24
